TPU v7x, 32 devices: a whole 2x2x4 slice. The times are simulated.
32 devices in a mesh: row: 4 (over y, x), col: 4 (over z), depth: 2 (over core).
Axes of the slice: x: 2, y: 2, z: 4, core: 2. Of those that a mesh axis runs over, the one named last changes fastest.
Arguments:
- features: bfloat16 [8192, 128], P(('row', 'col')), may hold values from -6 to 6
- self_weight: bfloat16 [128, 256], P(None, 'depth'), may hold values from -0.5 to 0.5
- neigh_weight: bfloat16 [128, 256], P(None, 'depth'), may hold values from -0.5 to 0.5
- bias: float32 [256], P('depth'), may hold values from -3 to 3
- cotangent: bfloat16 [8192, 256], P(('row', 'col'), 'depth'), may hold values from -6 to 6
- tile_values: bfloat16 [8192, 128, 128], P(('row', 'col', 'depth')), may hold values from -0.0625 to 0.0625
- tile_rows: int32 [32, 256], P(('row', 'col', 'depth')), may hold values from 0 to 15
- tile_cols: int32 [32, 256], P(('row', 'col', 'depth')), may hold values from 0 to 15
- tile_counts: int32 [32], P(('row', 'col', 'depth')), may hold values from 32 to 256, as said below
Outputs:
- output: bfloat16 [8192, 256], P(('row', 'col'), 'depth')
- grad_features: bfloat16 [8192, 128], P(('row', 'col', 'depth'))
- grad_self: float32 [128, 256], P(None, 'depth')
- grad_neigh: float32 [128, 256], P(None, 'depth')
- grad_bias: float32 [256], P('depth')
Inputs may be any that keep to these rules, and one draw needn't show every extreme that they name: `tile_rows`: a row block below 16. `tile_cols`: a column block below 16. `tile_counts`: each device's count is 256 divided by 1, 2, 4 or 8; some device has all 256 slots live.
All inputs are finite; a program needn't handle non-finite values.
Results may differ from a plain program's by a relative error of at most 0.0057.
Values may be sent and summed in bfloat16 or wider, within the bound.
A program may use at most 64 MiB of HBM per device.

v0:
```python
import jax
import jax.numpy as jnp
from jax import lax
from jax.sharding import PartitionSpec as P


def accumulate(
    tile_values,
    out_blocks,
    in_blocks,
    live_mask,
    source,
    block_count,
    forward,
    group_bound,
    group_size,
):
    block_size = tile_values.shape[1]
    hidden = source.shape[1]
    source_blocks = source.reshape(-1, block_size, hidden)

    def add_group(group_index, totals):
        offset = group_index * group_size
        tile_block = lax.dynamic_slice_in_dim(tile_values, offset, group_size, 0)
        out_index = lax.dynamic_slice_in_dim(out_blocks, offset, group_size, 0)
        in_index = lax.dynamic_slice_in_dim(in_blocks, offset, group_size, 0)
        alive = lax.dynamic_slice_in_dim(live_mask, offset, group_size, 0)
        if forward:
            product = jnp.einsum(
                "tij,tjh->tih",
                tile_block,
                source_blocks[in_index],
                preferred_element_type=jnp.float32,
            )
            target = out_index
        else:
            product = jnp.einsum(
                "tij,tih->tjh",
                tile_block,
                source_blocks[out_index],
                preferred_element_type=jnp.float32,
            )
            target = in_index
        product = jnp.where(alive[:, None, None], product, 0.0)
        return totals.at[target].add(product)

    totals = jnp.zeros((block_count, block_size, hidden), jnp.float32)
    totals = lax.fori_loop(0, group_bound, add_group, totals)
    return totals.reshape(block_count * block_size, hidden)


def body(
    features,
    self_weight,
    neigh_weight,
    bias,
    cotangent,
    tile_values,
    tile_rows,
    tile_cols,
    tile_counts,
):
    span_rows = features.shape[0]
    block_size = tile_values.shape[1]
    tile_slots = tile_values.shape[0]
    row_count = lax.axis_size("row")
    col_count = lax.axis_size("col")
    out_blocks = tile_rows[0]
    in_blocks = tile_cols[0]
    live_count = tile_counts[0]
    live_mask = jnp.arange(tile_slots, dtype=jnp.int32) < live_count
    group_size = 32
    group_bound = tile_slots // group_size
    transformed = jnp.dot(features, neigh_weight, preferred_element_type=jnp.float32).astype(
        jnp.bfloat16
    )
    transformed = lax.all_gather(transformed, "depth", axis=1, tiled=True)
    column_source = lax.all_gather(transformed, "row", axis=0, tiled=True)
    row_blocks = span_rows * col_count // block_size
    partial_value = accumulate(
        tile_values,
        out_blocks,
        in_blocks,
        live_mask,
        column_source,
        row_blocks,
        True,
        group_bound,
        group_size,
    )
    aggregated = lax.psum_scatter(partial_value, "depth", scatter_dimension=1, tiled=True)
    aggregated = lax.psum_scatter(aggregated, "col", scatter_dimension=0, tiled=True)
    preact = jnp.dot(features, self_weight, preferred_element_type=jnp.float32) + aggregated + bias
    gate_value = jax.nn.sigmoid(preact)
    output = (preact * gate_value).astype(jnp.bfloat16)
    grad_pre = (
        cotangent.astype(jnp.float32) * gate_value * (1.0 + preact * (1.0 - gate_value))
    ).astype(jnp.bfloat16)
    grad_rows = lax.all_gather(grad_pre, "col", axis=0, tiled=True)
    grad_rows = lax.all_gather(grad_rows, "depth", axis=1, tiled=True)
    column_blocks = span_rows * row_count // block_size
    grad_partial = accumulate(
        tile_values,
        out_blocks,
        in_blocks,
        live_mask,
        grad_rows,
        column_blocks,
        False,
        group_bound,
        group_size,
    )
    grad_partial = lax.psum_scatter(grad_partial, "depth", scatter_dimension=1, tiled=True)
    grad_transformed = lax.psum_scatter(
        grad_partial, "row", scatter_dimension=0, tiled=True
    ).astype(jnp.bfloat16)
    input_terms = jnp.dot(grad_pre, self_weight.T, preferred_element_type=jnp.float32) + jnp.dot(
        grad_transformed, neigh_weight.T, preferred_element_type=jnp.float32
    )
    grad_features = lax.psum_scatter(input_terms, "depth", scatter_dimension=0, tiled=True).astype(
        jnp.bfloat16
    )
    contract = (((0,), (0,)), ((), ()))
    self_local = lax.dot_general(features, grad_pre, contract, preferred_element_type=jnp.float32)
    neigh_local = lax.dot_general(
        features, grad_transformed, contract, preferred_element_type=jnp.float32
    )
    bias_local = jnp.sum(grad_pre.astype(jnp.float32), axis=0)
    grad_self, grad_neigh, grad_bias = lax.psum(
        (self_local, neigh_local, bias_local), ("row", "col")
    )
    grad_scale = 1.0 / jnp.sqrt(jnp.float32(span_rows * row_count * col_count))
    return (
        output,
        grad_features,
        grad_self * grad_scale,
        grad_neigh * grad_scale,
        grad_bias * grad_scale,
    )


def solution(mesh):
    placed = (
        P(("row", "col"), None),
        P(None, "depth"),
        P(None, "depth"),
        P("depth"),
        P(("row", "col"), "depth"),
        P(("row", "col", "depth"), None, None),
        P(("row", "col", "depth"), None),
        P(("row", "col", "depth"), None),
        P(("row", "col", "depth")),
    )
    return jax.shard_map(
        body,
        mesh=mesh,
        in_specs=placed,
        out_specs=(
            P(("row", "col"), "depth"),
            P(("row", "col", "depth"), None),
            P(None, "depth"),
            P(None, "depth"),
            P("depth"),
        ),
        check_vma=False,
    )
```

profile of v0, /device:TPU:0, one launch (start us, length us, event | category | flops | bytes accessed | tf_op | source)
XLA Modules:
  0.0 496.1 jit_solution(15493962222124298284)
XLA Ops:
  12.0 28.7 %all-gather.3.cloned.1.call-done = bf16[2048,256]{1,0:T(8,128)(2,1)} async-done(((bf16[512,256]{1,0:T(8,128)(2,1)}), bf16[2048,256]{1,0:T(8,128)(2,1)}) %all-gather.3.cloned.1.call-update) | async-done | bytes 1048592 | tf_op jit(solution)/shard_map/all_gather | solution.py:78
  41.9 106.0 %while.26 = (s32[]{:T(128)}, f32[16,128,256]{2,1,0:T(8,128)S(1)}, s32[256]{0:T(256)S(1)}, pred[256]{0:T(512)(128)(4,1)S(1)}, bf16[256,128,128]{2,1,0:T(8,128)(2,...) while((s32[]{:T(128)}, f32[16,128,256]{2,1,0:T(8,128)S(1)}, ...), condition=%wide.region_2.3_spmd, body=%wide.region_0.2_spmd.sunk | while | flops 270533824 | bytes 24122504 | solution.py:48
  48.6 6.5 %scatter_fusion = f32[16,128,256]{2,1,0:T(8,128)S(1)} fusion(f32[16,128,256]{2,1,0:T(8,128)S(1)} %get-tuple-element.412, s32[32]{0:T(128)S(1)} %get-tuple-element.389, f32[32,128,256]{2,1,0:T(8,128)} %convolution_select_fusion.4), kind=kCustom, calls=%fused_computation.2.clone.1 | custom fusion | flops 1048576 | bytes 12583040 | tf_op jit(solution)/shard_map/while/body/eval_jaxpr/scatter-add | solution.py:45
  61.9 6.5 %scatter_fusion = f32[16,128,256]{2,1,0:T(8,128)S(1)} fusion(f32[16,128,256]{2,1,0:T(8,128)S(1)} %get-tuple-element.412, s32[32]{0:T(128)S(1)} %get-tuple-element.389, f32[32,128,256]{2,1,0:T(8,128)} %convolution_select_fusion.4), kind=kCustom, calls=%fused_computation.2.clone.1 | custom fusion | flops 1048576 | bytes 12583040 | tf_op jit(solution)/shard_map/while/body/eval_jaxpr/scatter-add | solution.py:45
  75.1 6.5 %scatter_fusion = f32[16,128,256]{2,1,0:T(8,128)S(1)} fusion(f32[16,128,256]{2,1,0:T(8,128)S(1)} %get-tuple-element.412, s32[32]{0:T(128)S(1)} %get-tuple-element.389, f32[32,128,256]{2,1,0:T(8,128)} %convolution_select_fusion.4), kind=kCustom, calls=%fused_computation.2.clone.1 | custom fusion | flops 1048576 | bytes 12583040 | tf_op jit(solution)/shard_map/while/body/eval_jaxpr/scatter-add | solution.py:45
  88.4 6.5 %scatter_fusion = f32[16,128,256]{2,1,0:T(8,128)S(1)} fusion(f32[16,128,256]{2,1,0:T(8,128)S(1)} %get-tuple-element.412, s32[32]{0:T(128)S(1)} %get-tuple-element.389, f32[32,128,256]{2,1,0:T(8,128)} %convolution_select_fusion.4), kind=kCustom, calls=%fused_computation.2.clone.1 | custom fusion | flops 1048576 | bytes 12583040 | tf_op jit(solution)/shard_map/while/body/eval_jaxpr/scatter-add | solution.py:45
  101.6 6.5 %scatter_fusion = f32[16,128,256]{2,1,0:T(8,128)S(1)} fusion(f32[16,128,256]{2,1,0:T(8,128)S(1)} %get-tuple-element.412, s32[32]{0:T(128)S(1)} %get-tuple-element.389, f32[32,128,256]{2,1,0:T(8,128)} %convolution_select_fusion.4), kind=kCustom, calls=%fused_computation.2.clone.1 | custom fusion | flops 1048576 | bytes 12583040 | tf_op jit(solution)/shard_map/while/body/eval_jaxpr/scatter-add | solution.py:45
  114.9 6.5 %scatter_fusion = f32[16,128,256]{2,1,0:T(8,128)S(1)} fusion(f32[16,128,256]{2,1,0:T(8,128)S(1)} %get-tuple-element.412, s32[32]{0:T(128)S(1)} %get-tuple-element.389, f32[32,128,256]{2,1,0:T(8,128)} %convolution_select_fusion.4), kind=kCustom, calls=%fused_computation.2.clone.1 | custom fusion | flops 1048576 | bytes 12583040 | tf_op jit(solution)/shard_map/while/body/eval_jaxpr/scatter-add | solution.py:45
  128.1 6.5 %scatter_fusion = f32[16,128,256]{2,1,0:T(8,128)S(1)} fusion(f32[16,128,256]{2,1,0:T(8,128)S(1)} %get-tuple-element.412, s32[32]{0:T(128)S(1)} %get-tuple-element.389, f32[32,128,256]{2,1,0:T(8,128)} %convolution_select_fusion.4), kind=kCustom, calls=%fused_computation.2.clone.1 | custom fusion | flops 1048576 | bytes 12583040 | tf_op jit(solution)/shard_map/while/body/eval_jaxpr/scatter-add | solution.py:45
  141.4 6.5 %scatter_fusion = f32[16,128,256]{2,1,0:T(8,128)S(1)} fusion(f32[16,128,256]{2,1,0:T(8,128)S(1)} %get-tuple-element.412, s32[32]{0:T(128)S(1)} %get-tuple-element.389, f32[32,128,256]{2,1,0:T(8,128)} %convolution_select_fusion.4), kind=kCustom, calls=%fused_computation.2.clone.1 | custom fusion | flops 1048576 | bytes 12583040 | tf_op jit(solution)/shard_map/while/body/eval_jaxpr/scatter-add | solution.py:45
  149.3 9.7 %reduce-scatter.6.cloned.1.call-done = f32[2048,128]{1,0:T(8,128)} async-done(((f32[2048,256]{1,0:T(8,128)}), f32[2048,128]{1,0:T(8,128)}) %reduce-scatter.6.cloned.1.call-update) | async-done | bytes 1048592 | tf_op jit(solution)/shard_map/reduce_scatter | solution.py:91
  159.0 30.7 %reduce-scatter.8.cloned.1.call-done = f32[512,128]{1,0:T(8,128)} async-done(((f32[2048,128]{1,0:T(8,128)}), f32[512,128]{1,0:T(8,128)}) %reduce-scatter.8.cloned.1.call-update) | async-done | bytes 262160 | tf_op jit(solution)/shard_map/reduce_scatter | solution.py:92
  191.6 16.4 %all_gather.14 = bf16[2048,128]{1,0:T(8,128)(2,1)} all-gather(bf16[512,128]{1,0:T(8,128)(2,1)S(1)} %get-tuple-element.298), channel_id=1, replica_groups=mesh['row'=4,'col'=4,'depth'=2] {'col'}, dimensions={0}, use_global_device_ids=true | all-gather | bytes 655360 | tf_op jit(solution)/shard_map/all_gather | solution.py:99
  208.1 7.4 %all-gather.5.cloned.1.call-done = bf16[2048,256]{1,0:T(8,128)(2,1)} async-done(((bf16[2048,128]{1,0:T(8,128)(2,1)}), bf16[2048,256]{1,0:T(8,128)(2,1)}) %all-gather.5.cloned.1.call-update) | async-done | bytes 1048592 | tf_op jit(solution)/shard_map/all_gather | solution.py:100
  216.8 107.1 %while.27 = (s32[]{:T(128)}, f32[16,128,256]{2,1,0:T(8,128)S(1)}, s32[256]{0:T(256)S(1)}, pred[256]{0:T(512)(128)(4,1)S(1)}, bf16[256,128,128]{2,1,0:T(8,128)(2,...) while((s32[]{:T(128)}, f32[16,128,256]{2,1,0:T(8,128)S(1)}, ...), condition=%wide.region_7.8_spmd, body=%wide.region_5.7_spmd.sunk | while | flops 270533824 | bytes 24122504 | solution.py:48
  223.6 6.5 %scatter_fusion.1 = f32[16,128,256]{2,1,0:T(8,128)S(1)} fusion(f32[16,128,256]{2,1,0:T(8,128)S(1)} %get-tuple-element.445, s32[32]{0:T(128)S(1)} %get-tuple-element.398, f32[32,128,256]{2,1,0:T(8,128)} %convolution_select_fusion.5), kind=kCustom, calls=%fused_computation.3.clone.1 | custom fusion | flops 1048576 | bytes 12583040 | tf_op jit(solution)/shard_map/while/body/eval_jaxpr/scatter-add | solution.py:45
  232.3 4.7 convolution_select_fusion.5
  237.0 6.5 %scatter_fusion.1 = f32[16,128,256]{2,1,0:T(8,128)S(1)} fusion(f32[16,128,256]{2,1,0:T(8,128)S(1)} %get-tuple-element.445, s32[32]{0:T(128)S(1)} %get-tuple-element.398, f32[32,128,256]{2,1,0:T(8,128)} %convolution_select_fusion.5), kind=kCustom, calls=%fused_computation.3.clone.1 | custom fusion | flops 1048576 | bytes 12583040 | tf_op jit(solution)/shard_map/while/body/eval_jaxpr/scatter-add | solution.py:45
  245.7 4.7 convolution_select_fusion.5
  250.4 6.5 %scatter_fusion.1 = f32[16,128,256]{2,1,0:T(8,128)S(1)} fusion(f32[16,128,256]{2,1,0:T(8,128)S(1)} %get-tuple-element.445, s32[32]{0:T(128)S(1)} %get-tuple-element.398, f32[32,128,256]{2,1,0:T(8,128)} %convolution_select_fusion.5), kind=kCustom, calls=%fused_computation.3.clone.1 | custom fusion | flops 1048576 | bytes 12583040 | tf_op jit(solution)/shard_map/while/body/eval_jaxpr/scatter-add | solution.py:45
  263.8 6.5 %scatter_fusion.1 = f32[16,128,256]{2,1,0:T(8,128)S(1)} fusion(f32[16,128,256]{2,1,0:T(8,128)S(1)} %get-tuple-element.445, s32[32]{0:T(128)S(1)} %get-tuple-element.398, f32[32,128,256]{2,1,0:T(8,128)} %convolution_select_fusion.5), kind=kCustom, calls=%fused_computation.3.clone.1 | custom fusion | flops 1048576 | bytes 12583040 | tf_op jit(solution)/shard_map/while/body/eval_jaxpr/scatter-add | solution.py:45
  272.5 4.7 convolution_select_fusion.5
  277.2 6.5 %scatter_fusion.1 = f32[16,128,256]{2,1,0:T(8,128)S(1)} fusion(f32[16,128,256]{2,1,0:T(8,128)S(1)} %get-tuple-element.445, s32[32]{0:T(128)S(1)} %get-tuple-element.398, f32[32,128,256]{2,1,0:T(8,128)} %convolution_select_fusion.5), kind=kCustom, calls=%fused_computation.3.clone.1 | custom fusion | flops 1048576 | bytes 12583040 | tf_op jit(solution)/shard_map/while/body/eval_jaxpr/scatter-add | solution.py:45
  285.9 4.7 convolution_select_fusion.5
  290.6 6.5 %scatter_fusion.1 = f32[16,128,256]{2,1,0:T(8,128)S(1)} fusion(f32[16,128,256]{2,1,0:T(8,128)S(1)} %get-tuple-element.445, s32[32]{0:T(128)S(1)} %get-tuple-element.398, f32[32,128,256]{2,1,0:T(8,128)} %convolution_select_fusion.5), kind=kCustom, calls=%fused_computation.3.clone.1 | custom fusion | flops 1048576 | bytes 12583040 | tf_op jit(solution)/shard_map/while/body/eval_jaxpr/scatter-add | solution.py:45
  304.0 6.5 %scatter_fusion.1 = f32[16,128,256]{2,1,0:T(8,128)S(1)} fusion(f32[16,128,256]{2,1,0:T(8,128)S(1)} %get-tuple-element.445, s32[32]{0:T(128)S(1)} %get-tuple-element.398, f32[32,128,256]{2,1,0:T(8,128)} %convolution_select_fusion.5), kind=kCustom, calls=%fused_computation.3.clone.1 | custom fusion | flops 1048576 | bytes 12583040 | tf_op jit(solution)/shard_map/while/body/eval_jaxpr/scatter-add | solution.py:45
  317.3 6.5 %scatter_fusion.1 = f32[16,128,256]{2,1,0:T(8,128)S(1)} fusion(f32[16,128,256]{2,1,0:T(8,128)S(1)} %get-tuple-element.445, s32[32]{0:T(128)S(1)} %get-tuple-element.398, f32[32,128,256]{2,1,0:T(8,128)} %convolution_select_fusion.5), kind=kCustom, calls=%fused_computation.3.clone.1 | custom fusion | flops 1048576 | bytes 12583040 | tf_op jit(solution)/shard_map/while/body/eval_jaxpr/scatter-add | solution.py:45
  325.2 10.9 %reduce-scatter.10.cloned.1.call-done = f32[2048,128]{1,0:T(8,128)} async-done(((f32[2048,256]{1,0:T(8,128)}), f32[2048,128]{1,0:T(8,128)}) %reduce-scatter.10.cloned.1.call-update) | async-done | bytes 1048592 | tf_op jit(solution)/shard_map/reduce_scatter | solution.py:113
  337.2 30.8 %reduce-scatter.12.cloned.1.call-done = f32[512,128]{1,0:T(8,128)} async-done(((f32[2048,128]{1,0:T(8,128)}), f32[512,128]{1,0:T(8,128)}) %reduce-scatter.12.cloned.1.call-update) | async-done | bytes 262160 | tf_op jit(solution)/shard_map/reduce_scatter | solution.py:114
  371.8 41.0 %psum.23 = f32[128]{0:T(128)S(1)} all-reduce(f32[128]{0:T(128)S(1)} %get-tuple-element.297), channel_id=1, replica_groups=mesh['row'=4,'col'=4,'depth'=2] {'row','col'}, use_global_device_ids=true, to_apply=%region_14.15 | all-reduce | flops 128 | bytes 1024 | tf_op jit(solution)/shard_map/psum | solution.py:129
  413.3 65.4 %all-reduce.3.cloned.1.call-done = (f32[128,128]{0,1:T(8,128)}, f32[128,128]{0,1:T(8,128)}) async-done(((f32[128,128]{0,1:T(8,128)}, f32[128,128]{0,1:T(8,128)}), (f32[128,128]{0,1:T(8,128)}, f32[128,128]{0,1:T(8,128)})) %all-reduce.3.cloned.1.call-update) | async-done | bytes 131088 | tf_op jit(solution)/shard_map/psum | solution.py:129
  481.1 6.6 %reduce-scatter.14.cloned.1.call-done = f32[256,128]{1,0:T(8,128)} async-done(((f32[512,128]{1,0:T(8,128)}), f32[256,128]{1,0:T(8,128)}) %reduce-scatter.14.cloned.1.call-update) | async-done | bytes 131088 | tf_op jit(solution)/shard_map/reduce_scatter | solution.py:120
  (129 shorter events, 110.5 us)
Async XLA Ops:
  7.2 0.9 copy-start
  7.2 33.7 %copy-start.7 = (s32[1,256]{1,0:T(1,128)S(1)}, s32[1,256]{1,0:T(1,128)}, u32[]{:S(2)}) copy-start(s32[1,256]{1,0:T(1,128)} %param.19) | copy-start | bytes 3076
  7.2 33.7 %copy-start.8 = (s32[1,256]{1,0:T(1,128)S(1)}, s32[1,256]{1,0:T(1,128)}, u32[]{:S(2)}) copy-start(s32[1,256]{1,0:T(1,128)} %param.20) | copy-start | bytes 3076
  7.2 33.4 %all-gather.3.cloned.1.call-start = ((), (), s32[]{:S(2)}) async-start(), calls=%async_computation.5 | async-start | bytes 1310720 | tf_op jit(solution)/shard_map/all_gather | solution.py:78
  11.2 147.7 %reduce-scatter.6.cloned.1.call-start = ((), (), s32[]{:S(2)}) async-start(), calls=%async_computation.6 | async-start | bytes 3145728 | tf_op jit(solution)/shard_map/reduce_scatter | solution.py:91
  40.6 1.2 copy-start.4
  147.8 1.3 copy-start.2
  147.9 41.9 %copy-start.6 = (bf16[128,128]{1,0:T(8,128)(2,1)S(1)}, bf16[128,128]{1,0:T(8,128)(2,1)}, u32[]{:S(2)}) copy-start(bf16[128,128]{1,0:T(8,128)(2,1)} %param.14) | copy-start | bytes 98308
  147.9 41.9 %copy-start.9 = (bf16[512,128]{1,0:T(8,128)(2,1)S(1)}, bf16[512,128]{1,0:T(8,128)(2,1)}, u32[]{:S(2)}) copy-start(bf16[512,128]{1,0:T(8,128)(2,1)} %param.17) | copy-start | bytes 393220
  147.9 41.8 %copy-start.10 = (f32[128]{0:T(128)S(1)}, f32[128]{0:T(128)}, u32[]{:S(2)}) copy-start(f32[128]{0:T(128)} %param.16) | copy-start | bytes 1540
  149.2 40.5 %reduce-scatter.8.cloned.1.call-start = ((), (), s32[]{:S(2)}) async-start(), calls=%async_computation.7 | async-start | bytes 1310720 | tf_op jit(solution)/shard_map/reduce_scatter | solution.py:92
  159.0 56.5 %all-gather.5.cloned.1.call-start = ((), (), s32[]{:S(2)}) async-start(), calls=%async_computation.8 | async-start | bytes 1572864 | tf_op jit(solution)/shard_map/all_gather | solution.py:100
  208.1 128.0 %reduce-scatter.10.cloned.1.call-start = ((), (), s32[]{:S(2)}) async-start(), calls=%async_computation.9 | async-start | bytes 3145728 | tf_op jit(solution)/shard_map/reduce_scatter | solution.py:113
  215.5 1.2 copy-start.3
  323.8 1.3 copy-start.1
  323.8 46.1 %copy-start.5 = (bf16[128,128]{1,0:T(8,128)(2,1)S(1)}, bf16[128,128]{1,0:T(8,128)(2,1)}, u32[]{:S(2)}) copy-start(bf16[128,128]{1,0:T(8,128)(2,1)} %param.15) | copy-start | bytes 98308
  325.2 42.8 %reduce-scatter.12.cloned.1.call-start = ((), (), s32[]{:S(2)}) async-start(), calls=%async_computation.10 | async-start | bytes 1310720 | tf_op jit(solution)/shard_map/reduce_scatter | solution.py:114
  336.1 142.6 %all-reduce.3.cloned.1.call-start = ((), (), s32[]{:S(2)}) async-start(), calls=%async_computation.12 | async-start | bytes 262144 | tf_op jit(solution)/shard_map/psum | solution.py:129
  369.8 117.9 %reduce-scatter.14.cloned.1.call-start = ((), (), s32[]{:S(2)}) async-start(), calls=%async_computation.11 | async-start | bytes 393216 | tf_op jit(solution)/shard_map/reduce_scatter | solution.py:120
Sparse Core Ops, SparseCore 0:
  11.4 29.2 all-gather.2
  149.3 9.6 reduce-scatter.5
  161.4 28.2 reduce-scatter.7
  208.2 7.3 all-gather.4
  325.3 10.7 reduce-scatter.9
  339.1 28.8 reduce-scatter.11
  374.1 104.5 all-reduce.2
  480.9 6.7 reduce-scatter.13
where the time goes:
time: 498 us; the launch traced here: 496 us
  waiting for transfers between devices  190 us (38%)
  other arithmetic  108 us (22%)
  matrix products  81.6 us (16%)
  blocking collectives  59.6 us (12%)
  local copies, waits for them, and re-layouts  40.8 us (8%)
  between operations  14.9 us (3%)
    scatter-add x16, other arithmetic, add_group(): return totals.at[target].add(product)  104 us
    psum x1, waiting for transfers between devices, body(): lax.psum((self_local, neigh_local, bias_local), ('row', 'col'))  65.4 us
    psum x1, blocking collectives, body(): lax.psum((self_local, neigh_local, bias_local), ('row', 'col'))  41 us
    dot_general x8, matrix products, add_group(): jnp.einsum('tij,tih->tjh', tile_block, source_blocks[out_index], preferre...  37.6 us
    dot_general x8, matrix products, add_group(): jnp.einsum('tij,tjh->tih', tile_block, source_blocks[in_index], preferred...  36.5 us
    reduce_scatter x1, waiting for transfers between devices, body(): lax.psum_scatter(grad_partial, 'row', scatter_dimension=0, tiled=True)  30.8 us
    reduce_scatter x1, waiting for transfers between devices, body(): lax.psum_scatter(aggregated, 'col', scatter_dimension=0, tiled=True)  30.7 us
    all_gather x1, waiting for transfers between devices, body(): column_source = lax.all_gather(transformed, 'row', axis=0, tiled=True)  28.7 us
  transfers between devices with their start and end apart: 8, of which 8 were waited for; matrix products, arithmetic and copies ran while one was open for 1% of the time, Pallas kernels for 0%

commit v1 on v0

v1 whole, which is shorter than its diff:
```python
import functools

import jax
import jax.numpy as jnp
from jax import lax
from jax.experimental import pallas as pl
from jax.experimental.pallas import tpu as pltpu
from jax.sharding import PartitionSpec as P

BF = jnp.bfloat16
F32 = jnp.float32


def dot(a, b, ca=1, cb=0):
    return lax.dot_general(a, b, (((ca,), (cb,)), ((), ())), preferred_element_type=F32)


def peer_order(n):
    return sorted(range(1, n), key=lambda k: (abs(2 * k - n), k))


def kernel(
    dims,
    feat,
    ws,
    wn,
    bias,
    cot,
    rows_ref,
    cols_ref,
    counts,
    tiles_hbm,
    out,
    gfeat,
    wout,
    tiles,
    run,
    dense,
    f_all,
    wsx,
    wnx,
    biasb,
    biasx,
    cotx,
    idx_v,
    idx_s,
    p_own,
    p_mate,
    p_x,
    s_b,
    z_x,
    o_mate,
    u_all,
    g_acc,
    g_own,
    g_mate,
    g_x,
    gs_b,
    gz_x,
    w_part,
    w_x,
    w_rx,
    w_2,
    w_cx,
    v_t,
    tile_sem,
    loc_sem,
    send_sem,
    recv_sem,
):
    nr, nc, n, block, slots, chunks = dims
    f = feat.shape[1]
    hh = ws.shape[1]
    half = n // 2
    rb = nc * n // block
    cb = nr * n // block
    r, c, d = lax.axis_index("row"), lax.axis_index("col"), lax.axis_index("depth")
    mate = (r, c, 1 - d)

    def row_peer(k):
        return lax.rem(r + k, nr)

    def col_peer(k):
        return lax.rem(c + k, nc)

    made = []

    def send(src, dst, device):
        i = len(made)
        copy = pltpu.make_async_remote_copy(
            src_ref=src,
            dst_ref=dst,
            send_sem=send_sem.at[i],
            recv_sem=recv_sem.at[i],
            device_id=device,
            device_id_type=pl.DeviceIdType.MESH,
        )
        copy.start()
        made.append(copy)
        return copy

    per = slots // chunks
    loads = []
    for i in range(chunks):
        part = pl.ds(i * per, per)
        load = pltpu.make_async_copy(tiles_hbm.at[part], tiles.at[part], tile_sem.at[i])
        load.start()
        loads.append(load)

    barrier = pltpu.get_barrier_semaphore()
    peers = [mate]
    peers += [(row_peer(k), c, d) for k in range(1, nr)]
    peers += [(r, col_peer(k), d) for k in range(1, nc)]
    for p in peers:
        pl.semaphore_signal(barrier, inc=1, device_id=p, device_id_type=pl.DeviceIdType.MESH)

    own_rows = pl.ds(pl.multiple_of(d * half, half), half)
    mate_rows = pl.ds(pl.multiple_of((1 - d) * half, half), half)
    live = counts[0]
    lane = lax.broadcasted_iota(jnp.int32, (slots, slots), 1)
    sub = lax.broadcasted_iota(jnp.int32, (slots, slots), 0)
    pos_row = jnp.broadcast_to(rows_ref[...] * cb + cols_ref[...], (slots, slots))
    pos_row = jnp.where(lane < live, pos_row, rb * cb)
    key_row = pos_row * slots + lane
    key_col = jnp.sum(jnp.where(lane == sub, key_row, 0), axis=1, keepdims=True)
    pos_col = jnp.sum(jnp.where(lane == sub, pos_row, 0), axis=1, keepdims=True)
    rank = jnp.sum((key_row < key_col).astype(jnp.int32), axis=1, keepdims=True)
    hit = rank == lane
    idx_v[0:1, 0:slots] = jnp.sum(jnp.where(hit, sub, 0), axis=0, keepdims=True)
    idx_v[1:2, 0:slots] = jnp.sum(jnp.where(hit, pos_col, 0), axis=0, keepdims=True)
    places = lax.broadcasted_iota(jnp.int32, (slots, rb * cb), 1)
    upto = jnp.sum((pos_col <= places).astype(jnp.int32), axis=0, keepdims=True)
    below = jnp.sum((pos_col < places).astype(jnp.int32), axis=0, keepdims=True)
    idx_v[2:3, 0 : rb * cb] = jnp.where(upto > below, upto - 1, slots)
    to_smem = pltpu.make_async_copy(idx_v, idx_s, loc_sem.at[0])
    to_smem.start()

    pl.semaphore_wait(barrier, len(peers))
    my_f = pl.ds(pl.multiple_of(r * n, n), n)
    biasb[...] = jnp.broadcast_to(bias[...], biasb.shape)
    feat_c = [send(feat, f_all.at[my_f], (row_peer(k), c, d)) for k in peer_order(nr)]
    early = [
        send(ws, wsx, mate),
        send(wn, wnx, mate),
        send(cot.at[mate_rows], cotx, mate),
        send(biasb, biasx, mate),
    ]
    f_all[my_f, :] = feat[...]
    run[slots] = jnp.zeros((block, block), BF)
    w_part[...] = jnp.zeros_like(w_part)
    to_smem.wait()
    for load in loads:
        load.wait()

    def merge(k, acc):
        same = idx_s[1, k] == idx_s[1, jnp.maximum(k - 1, 0)]
        acc = jnp.where(same, acc, 0.0) + tiles[idx_s[0, k]].astype(F32)
        run[k] = acc.astype(BF)
        return acc

    lax.fori_loop(0, slots, merge, jnp.zeros((block, block), F32), unroll=4)

    def place(i, carry):
        at = pl.ds(pl.multiple_of(i * block, block), block)
        for j in range(cb):
            dense[at, j * block : (j + 1) * block] = run[idx_s[2, i * cb + j]]
        return carry

    lax.fori_loop(0, rb, place, 0)

    for copy in feat_c:
        copy.wait_recv()

    def rows_at(owner, part):
        return pl.ds(pl.multiple_of(owner * n + part * half, half), half)

    x_c, z_c = {}, {}

    def finish(k):
        x_c[k].wait_recv()
        total = p_own[k] + p_x[k]
        if k == 0:
            p_own[0] = total
        else:
            s_b[k] = total.astype(BF)
            z_c[k] = send(s_b.at[k], z_x.at[k], (r, col_peer(k), d))

    order = peer_order(nc) + [0]
    for i, k in enumerate(order):
        owner = col_peer(k)
        p_mate[k] = dot(dense[rows_at(owner, 1 - d), :], f_all[...])
        x_c[k] = send(p_mate.at[k], p_x.at[k], mate)
        p_own[k] = dot(dense[rows_at(owner, d), :], f_all[...])
        if i:
            finish(order[i - 1])
    finish(order[-1])
    for copy in early:
        copy.wait_recv()
    f_own = feat[own_rows, :]
    agg = p_own[0]
    for k in peer_order(nc):
        z_c[k].wait_recv()
        agg = agg + z_x[k].astype(F32)

    hi = agg.astype(BF)
    lo = (agg - hi.astype(F32)).astype(BF)
    weights = [(ws[...], wn[...]), (wsx[...], wnx[...])]
    biases = [biasb[0:1, :], biasx[0:1, :]]
    cots = [cot[own_rows, :], cotx[...]]
    grads = []
    u_t = v = None
    for e in range(2):
        w_s, w_n = weights[e]
        pre = dot(f_own, w_s) + dot(hi, w_n) + dot(lo, w_n) + biases[e]
        gate = jax.nn.sigmoid(pre)
        value = (pre * gate).astype(BF)
        if e == 0:
            out[own_rows, :] = value
        else:
            o_mate[...] = value
        g = (cots[e].astype(F32) * gate * (1.0 + pre * (1.0 - gate))).astype(BF)
        grads.append(g)
        term = dot(w_n, g, 1, 1)
        u_t = term if u_t is None else u_t + term
    u_all[0, 0] = u_t.astype(BF)
    u_m = send(u_all.at[0, 0], u_all.at[0, 1], mate)
    u_c = {k: send(u_all.at[0, 0], u_all.at[k, 0], (r, col_peer(k), d)) for k in peer_order(nc)}
    out_c = send(o_mate, out.at[own_rows], mate)
    for e in (1, 0):
        g = grads[e]
        w_part[e, 0:f, :] = dot(f_own, g, 0, 0)
        w_part[e, f : 2 * f, :] = dot(hi, g, 0, 0)
        total = jnp.sum(g.astype(F32), axis=0, keepdims=True)
        w_part[e, 2 * f : 2 * f + 8, :] = jnp.broadcast_to(total, (8, hh))
        if e == 1:
            w_c = send(w_part.at[1], w_x, mate)
    v_t[...] = dot(weights[0][0], grads[0], 1, 1) + dot(weights[1][0], grads[1], 1, 1)

    def add_rows(k, e, first):
        owner = lax.rem(c - k + nc, nc)
        at = rows_at(owner, d if e == 0 else 1 - d)
        for q in range(nr):
            for h in range(2):
                col = q * n + h * half
                term = dot(u_all[k, e], dense[at, col : col + half])
                g_acc[q, h] = term if first else g_acc[q, h] + term

    add_rows(0, 0, True)

    w_rows = w_x.shape[0]
    wr = w_rows // nr
    wc = wr // nc
    w_c.wait_recv()
    w_part[0] = w_part[0] + w_x[...]
    wr_c = []
    for k in range(1, nr):
        at = pl.ds(pl.multiple_of(row_peer(k) * wr, 8), wr)
        wr_c.append(send(w_part.at[0, at], w_rx.at[k], (row_peer(k), c, d)))

    u_m.wait_recv()
    add_rows(0, 1, False)

    for copy in wr_c:
        copy.wait_recv()
    total = w_part[0, pl.ds(pl.multiple_of(r * wr, 8), wr), :]
    for k in range(1, nr):
        total = total + w_rx[k]
    w_2[...] = total
    wc_c = []
    for k in range(1, nc):
        at = pl.ds(pl.multiple_of(col_peer(k) * wc, 8), wc)
        wc_c.append(send(w_2.at[at], w_cx.at[k], (r, col_peer(k), d)))

    fwd_c = {}
    for k in reversed(peer_order(nc)):
        u_c[k].wait_recv()
        fwd_c[k] = send(u_all.at[k, 0], u_all.at[k, 1], mate)
        add_rows(k, 0, False)

    for copy in wc_c:
        copy.wait_recv()
    total = w_2[pl.ds(pl.multiple_of(c * wc, 8), wc), :]
    for k in range(1, nc):
        total = total + w_cx[k]
    mine = pl.ds(pl.multiple_of(r * wr + c * wc, 8), wc)
    wout[mine, :] = total * (1.0 / jnp.sqrt(jnp.full((1, 1), nr * nc * n, F32)))
    wg_c = [send(wout.at[mine], wout.at[mine], (r, col_peer(k), d)) for k in range(1, nc)]

    for copy in fwd_c.values():
        copy.wait_recv()

    def last_rows(owner, part):
        col = pl.ds(pl.multiple_of(owner * n + part * half, half), half)
        total = g_acc[owner, part]
        for k in peer_order(nc):
            at = rows_at(lax.rem(c - k + nc, nc), 1 - d)
            total = total + dot(u_all[k, 1], dense[at, col])
        return total

    gx_c, gz_c = {}, {}

    def finish_back(k):
        gx_c[k].wait_recv()
        total = g_own[k] + g_x[k]
        if k == 0:
            g_own[0] = total
        else:
            gs_b[k] = total.astype(BF)
            gz_c[k] = send(gs_b.at[k], gz_x.at[k], (row_peer(k), c, d))

    order = peer_order(nr) + [0]
    for i, k in enumerate(order):
        owner = row_peer(k)
        g_mate[k] = last_rows(owner, 1 - d)
        gx_c[k] = send(g_mate.at[k], g_x.at[k], mate)
        g_own[k] = last_rows(owner, d)
        if i:
            finish_back(order[i - 1])
    finish_back(order[-1])

    for copy in wg_c:
        copy.wait_recv()
    whole = pl.ds(pl.multiple_of(r * wr, 8), wr)
    ag_c = [send(wout.at[whole], wout.at[whole], (row_peer(k), c, d)) for k in range(1, nr)]

    total = v_t[...] + g_own[0]
    for k in peer_order(nr):
        gz_c[k].wait_recv()
        total = total + gz_x[k].astype(F32)
    gfeat[...] = total.T.astype(BF)

    out_c.wait_recv()
    for copy in ag_c:
        copy.wait_recv()
    for copy in made:
        copy.wait_send()


def body(mesh, features, self_weight, neigh_weight, bias, cotangent, tile_values, tile_rows, tile_cols, tile_counts):
    nr, nc, nd = mesh.shape["row"], mesh.shape["col"], mesh.shape["depth"]
    assert nd == 2
    n, f = features.shape
    hh = self_weight.shape[1]
    slots, block, _ = tile_values.shape
    half = n // nd
    rb, cb = nc * n // block, nr * n // block
    unit = nr * nc * 8
    w_rows = -(-(2 * f + 8) // unit) * unit
    chunks = 8
    width = max(slots, rb * cb)
    copies = 12 + 5 * nr + 6 * nc
    vmem = pl.BlockSpec(memory_space=pltpu.VMEM)
    dims = (nr, nc, n, block, slots, chunks)
    out, gfeat, wout = pl.pallas_call(
        functools.partial(kernel, dims),
        out_shape=(
            jax.ShapeDtypeStruct((n, hh), BF),
            jax.ShapeDtypeStruct((half, f), BF),
            jax.ShapeDtypeStruct((w_rows, hh), F32),
        ),
        in_specs=[vmem] * 7
        + [pl.BlockSpec(memory_space=pltpu.SMEM), pl.BlockSpec(memory_space=pl.ANY)],
        out_specs=(vmem, vmem, vmem),
        scratch_shapes=[
            pltpu.VMEM((slots, block, block), BF),
            pltpu.VMEM((slots + 1, block, block), BF),
            pltpu.VMEM((rb * block, cb * block), BF),
            pltpu.VMEM((nr * n, f), BF),
            pltpu.VMEM((f, hh), BF),
            pltpu.VMEM((f, hh), BF),
            pltpu.VMEM((8, hh), F32),
            pltpu.VMEM((8, hh), F32),
            pltpu.VMEM((half, hh), BF),
            pltpu.VMEM((8, width), jnp.int32),
            pltpu.SMEM((8, width), jnp.int32),
            pltpu.VMEM((nc, half, f), F32),
            pltpu.VMEM((nc, half, f), F32),
            pltpu.VMEM((nc, half, f), F32),
            pltpu.VMEM((nc, half, f), BF),
            pltpu.VMEM((nc, half, f), BF),
            pltpu.VMEM((half, hh), BF),
            pltpu.VMEM((nc, 2, f, half), BF),
            pltpu.VMEM((nr, 2, f, half), F32),
            pltpu.VMEM((nr, f, half), F32),
            pltpu.VMEM((nr, f, half), F32),
            pltpu.VMEM((nr, f, half), F32),
            pltpu.VMEM((nr, f, half), BF),
            pltpu.VMEM((nr, f, half), BF),
            pltpu.VMEM((2, w_rows, hh), F32),
            pltpu.VMEM((w_rows, hh), F32),
            pltpu.VMEM((nr, w_rows // nr, hh), F32),
            pltpu.VMEM((w_rows // nr, hh), F32),
            pltpu.VMEM((nc, w_rows // nr // nc, hh), F32),
            pltpu.VMEM((f, half), F32),
            pltpu.SemaphoreType.DMA((chunks,)),
            pltpu.SemaphoreType.DMA((1,)),
            pltpu.SemaphoreType.DMA((copies,)),
            pltpu.SemaphoreType.DMA((copies,)),
        ],
        compiler_params=pltpu.CompilerParams(
            collective_id=0, has_side_effects=True, vmem_limit_bytes=62 * 1024 * 1024
        ),
        name="sage_layer",
    )(
        features,
        self_weight,
        neigh_weight,
        bias.reshape(1, hh),
        cotangent,
        tile_rows,
        tile_cols,
        tile_counts,
        tile_values,
    )
    return out, gfeat, wout[:f], wout[f : 2 * f], wout[2 * f]


def solution(mesh):
    placed = (
        P(("row", "col"), None),
        P(None, "depth"),
        P(None, "depth"),
        P("depth"),
        P(("row", "col"), "depth"),
        P(("row", "col", "depth"), None, None),
        P(("row", "col", "depth"), None),
        P(("row", "col", "depth"), None),
        P(("row", "col", "depth")),
    )
    return jax.shard_map(
        functools.partial(body, mesh),
        mesh=mesh,
        in_specs=placed,
        out_specs=(
            P(("row", "col"), "depth"),
            P(("row", "col", "depth"), None),
            P(None, "depth"),
            P(None, "depth"),
            P("depth"),
        ),
        check_vma=False,
    )
```

time: 498 us -> 51 us (0.10)
  waiting for transfers between devices: 190 us -> 0 us
  other arithmetic: 108 us -> 0 us
  matrix products: 81.6 us -> 0 us
  blocking collectives: 59.6 us -> 0 us
  Pallas kernels: 0 us -> 43.7 us
  local copies, waits for them, and re-layouts: 40.8 us -> 5.75 us
  between operations: 14.9 us -> 1.29 us
    scatter-add x16 -> x0, other arithmetic: 104 us -> none  [add_group(): return totals.at[target].add(product)]
    reduce_scatter x5 -> x0, waiting for transfers between devices: 88.7 us -> none  [the longest x1 30.8 us: body(): lax.psum_scatter(grad_partial, 'row', scatter_dimension=0, tiled=True)]
    dot_general x22 -> x0, matrix products: 81.6 us -> none  [the longest x8 37.6 us: add_group(): jnp.einsum('tij,tih->tjh', tile_block, source_blocks[out_index], preferre...]
    psum x1 -> x0, waiting for transfers between devices: 65.4 us -> none  [body(): lax.psum((self_local, neigh_local, bias_local), ('row', 'col'))]
    pallas_call x0 -> x1, Pallas kernels: none -> 43.7 us  [body(): pl.pallas_call(functools.partial(kernel, dims), out_shape=(jax.ShapeDtype...]
    psum x1 -> x0, blocking collectives: 41 us -> none  [body(): lax.psum((self_local, neigh_local, bias_local), ('row', 'col'))]
    all_gather x2 -> x0, waiting for transfers between devices: 36.1 us -> none  [the longest x1 28.7 us: body(): column_source = lax.all_gather(transformed, 'row', axis=0, tiled=True)]
    gather x16 -> x0, local copies, waits for them, and re-layouts: 32.2 us -> none  [the longest x8 16.1 us: add_group(): source_blocks[in_index]]
  transfers between devices with their start and end apart: 8 -> 0, of which waited for: 8 -> 0; matrix products, arithmetic and copies ran while one was open for 1% -> 0% of each run, Pallas kernels for 0% -> 0%
where the time goes in v1:
time: 51 us; the launch traced here: 50.7 us
  Pallas kernels  43.7 us (86%)
  local copies, waits for them, and re-layouts  5.75 us (11%)
  between operations  1.29 us (3%)
    pallas_call x1, Pallas kernels, body(): pl.pallas_call(functools.partial(kernel, dims), out_shape=(jax.ShapeDtype...  43.7 us
    unnamed x2, local copies, waits for them, and re-layouts  3.04 us
    slice x1, local copies, waits for them, and re-layouts, body(): return (out, gfeat, wout[:f], wout[f:2 * f], wout[2 * f])  1.53 us
    squeeze x1, local copies, waits for them, and re-layouts, body(): return (out, gfeat, wout[:f], wout[f:2 * f], wout[2 * f])  1.18 us

profile of v1, /device:TPU:0, one launch (start us, length us, event | category | flops | bytes accessed | tf_op | source)
XLA Modules:
  0.0 50.7 jit_solution(14046781125115587330)
XLA Ops:
  1.3 43.7 %sage_layer.1 = (bf16[512,128]{1,0:T(8,128)(2,1)}, bf16[256,128]{1,0:T(8,128)(2,1)}, f32[384,128]{1,0:T(8,128)}) custom-call(bf16[512,128]{1,0:T(8,128)(2,1)} %feat.1, bf16[128,128]{1,0:T(8,128)(2,1)} %ws.1, bf16[128,128]{1,0:T(8,128)(2,1)} %wn.1, f32[1,128]{1,0:T(1,128)} %bitcast.3, bf16[512,128]{1,0:T(8,128)(2,1)} %cot.1, s32[1,256]{1,0:T(1,128)} %rows_ref.1, ...), custom_call_target="tpu_custom_call" | custom-call | tf_op jit(solution)/shard_map/sage_layer/pallas_call | solution.py:354
  45.0 1.5 %fusion = (f32[128,128]{1,0:T(8,128)}, f32[128,128]{1,0:T(8,128)}) fusion(f32[384,128]{1,0:T(8,128)} %get-tuple-element.10), kind=kLoop, calls=%fused_computation.1 | loop fusion | bytes 262144 | tf_op jit(solution)/shard_map/slice | solution.py:415
  46.5 1.2 %slice_bitcast_fusion = f32[128]{0:T(128)} fusion(f32[384,128]{1,0:T(8,128)} %get-tuple-element.10), kind=kLoop, calls=%fused_computation | loop fusion | bytes 1024 | tf_op jit(solution)/shard_map/squeeze | solution.py:415
  47.7 1.6 %copy.17 = bf16[512,128]{1,0:T(8,128)(2,1)} copy(bf16[512,128]{1,0:T(8,128)(2,1)} %get-tuple-element.18) | data formatting | bytes 262144
  49.3 1.5 %copy.18 = bf16[256,128]{1,0:T(8,128)(2,1)} copy(bf16[256,128]{1,0:T(8,128)(2,1)} %get-tuple-element.19) | data formatting | bytes 131072

commit v2 on v1

--- a/solution.py
+++ b/solution.py
@@ -21,11 +21,11 @@
 
 def kernel(
     dims,
-    feat,
-    ws,
-    wn,
+    feat_hbm,
+    ws_hbm,
+    wn_hbm,
     bias,
-    cot,
+    cot_hbm,
     rows_ref,
     cols_ref,
     counts,
@@ -35,8 +35,10 @@
     wout,
     tiles,
     run,
-    dense,
     f_all,
+    ws,
+    wn,
+    cot,
     wsx,
     wnx,
     biasb,
@@ -49,6 +51,7 @@
     p_x,
     s_b,
     z_x,
+    o_own,
     o_mate,
     u_all,
     g_acc,
@@ -63,13 +66,14 @@
     w_2,
     w_cx,
     v_t,
+    pre_s,
     tile_sem,
     loc_sem,
     send_sem,
     recv_sem,
 ):
     nr, nc, n, block, slots, chunks = dims
-    f = feat.shape[1]
+    f = feat_hbm.shape[1]
     hh = ws.shape[1]
     half = n // 2
     rb = nc * n // block
@@ -107,6 +111,26 @@
         load.start()
         loads.append(load)
 
+    my_f = pl.ds(pl.multiple_of(r * n, n), n)
+    own_rows = pl.ds(pl.multiple_of(d * half, half), half)
+    mate_rows = pl.ds(pl.multiple_of((1 - d) * half, half), half)
+
+    def f_rows(k):
+        at = lax.rem(r - k + nr, nr) * n + d * half
+        return pl.ds(pl.multiple_of(at, half), half)
+
+    def bring(i, src, dst):
+        load = pltpu.make_async_copy(src, dst, loc_sem.at[i])
+        load.start()
+        return load
+
+    brought = [
+        bring(0, feat_hbm, f_all.at[my_f]),
+        bring(1, ws_hbm, ws),
+        bring(2, wn_hbm, wn),
+        bring(3, cot_hbm.at[own_rows], cot),
+    ]
+
     barrier = pltpu.get_barrier_semaphore()
     peers = [mate]
     peers += [(row_peer(k), c, d) for k in range(1, nr)]
@@ -114,8 +138,6 @@
     for p in peers:
         pl.semaphore_signal(barrier, inc=1, device_id=p, device_id_type=pl.DeviceIdType.MESH)
 
-    own_rows = pl.ds(pl.multiple_of(d * half, half), half)
-    mate_rows = pl.ds(pl.multiple_of((1 - d) * half, half), half)
     live = counts[0]
     lane = lax.broadcasted_iota(jnp.int32, (slots, slots), 1)
     sub = lax.broadcasted_iota(jnp.int32, (slots, slots), 0)
@@ -132,20 +154,21 @@
     upto = jnp.sum((pos_col <= places).astype(jnp.int32), axis=0, keepdims=True)
     below = jnp.sum((pos_col < places).astype(jnp.int32), axis=0, keepdims=True)
     idx_v[2:3, 0 : rb * cb] = jnp.where(upto > below, upto - 1, slots)
-    to_smem = pltpu.make_async_copy(idx_v, idx_s, loc_sem.at[0])
+    to_smem = pltpu.make_async_copy(idx_v, idx_s, loc_sem.at[4])
     to_smem.start()
 
     pl.semaphore_wait(barrier, len(peers))
-    my_f = pl.ds(pl.multiple_of(r * n, n), n)
     biasb[...] = jnp.broadcast_to(bias[...], biasb.shape)
-    feat_c = [send(feat, f_all.at[my_f], (row_peer(k), c, d)) for k in peer_order(nr)]
+    feat_c = {
+        k: send(feat_hbm.at[own_rows], f_all.at[f_rows(0)], (row_peer(k), c, d))
+        for k in peer_order(nr)
+    }
     early = [
-        send(ws, wsx, mate),
-        send(wn, wnx, mate),
-        send(cot.at[mate_rows], cotx, mate),
+        send(ws_hbm, wsx, mate),
+        send(wn_hbm, wnx, mate),
+        send(cot_hbm.at[mate_rows], cotx, mate),
         send(biasb, biasx, mate),
     ]
-    f_all[my_f, :] = feat[...]
     run[slots] = jnp.zeros((block, block), BF)
     w_part[...] = jnp.zeros_like(w_part)
     to_smem.wait()
@@ -158,21 +181,34 @@
         run[k] = acc.astype(BF)
         return acc
 
-    lax.fori_loop(0, slots, merge, jnp.zeros((block, block), F32), unroll=4)
-
-    def place(i, carry):
-        at = pl.ds(pl.multiple_of(i * block, block), block)
-        for j in range(cb):
-            dense[at, j * block : (j + 1) * block] = run[idx_s[2, i * cb + j]]
-        return carry
-
-    lax.fori_loop(0, rb, place, 0)
-
-    for copy in feat_c:
+    acc = jnp.zeros((block, block), F32)
+    acc = lax.fori_loop(0, slots // 2, merge, acc, unroll=8)
+    pair_c = []
+    for k in peer_order(nr):
+        feat_c[k].wait_recv()
+        pair_c.append(send(f_all.at[f_rows(k)], f_all.at[f_rows(k)], mate))
+    lax.fori_loop(slots // 2, slots, merge, acc, unroll=8)
+
+    def merged(first_row, first_col, height, width):
+        lines = []
+        for i in range(height):
+            at = (first_row + i) * cb + first_col
+            line = [run[idx_s[2, at + j]] for j in range(width)]
+            lines.append(jnp.concatenate(line, axis=1))
+        return jnp.concatenate(lines, axis=0)
+
+    for load in brought:
+        load.wait()
+    for copy in pair_c:
         copy.wait_recv()
 
+    hb = half // block
+
     def rows_at(owner, part):
-        return pl.ds(pl.multiple_of(owner * n + part * half, half), half)
+        return (owner * 2 + part) * hb
+
+    def product(owner, part):
+        return dot(merged(rows_at(owner, part), 0, hb, cb), f_all[...])
 
     x_c, z_c = {}, {}
 
@@ -188,15 +224,19 @@
     order = peer_order(nc) + [0]
     for i, k in enumerate(order):
         owner = col_peer(k)
-        p_mate[k] = dot(dense[rows_at(owner, 1 - d), :], f_all[...])
+        p_mate[k] = product(owner, 1 - d)
         x_c[k] = send(p_mate.at[k], p_x.at[k], mate)
-        p_own[k] = dot(dense[rows_at(owner, d), :], f_all[...])
+        p_own[k] = product(owner, d)
         if i:
             finish(order[i - 1])
     finish(order[-1])
     for copy in early:
         copy.wait_recv()
-    f_own = feat[own_rows, :]
+    f_own = f_all[f_rows(0), :]
+    weights = [(ws[...], wn[...]), (wsx[...], wnx[...])]
+    biases = [biasb[0:1, :], biasx[0:1, :]]
+    for e in range(2):
+        pre_s[e] = dot(f_own, weights[e][0]) + biases[e]
     agg = p_own[0]
     for k in peer_order(nc):
         z_c[k].wait_recv()
@@ -204,18 +244,16 @@
 
     hi = agg.astype(BF)
     lo = (agg - hi.astype(F32)).astype(BF)
-    weights = [(ws[...], wn[...]), (wsx[...], wnx[...])]
-    biases = [biasb[0:1, :], biasx[0:1, :]]
-    cots = [cot[own_rows, :], cotx[...]]
+    cots = [cot[...], cotx[...]]
     grads = []
     u_t = v = None
     for e in range(2):
-        w_s, w_n = weights[e]
-        pre = dot(f_own, w_s) + dot(hi, w_n) + dot(lo, w_n) + biases[e]
+        w_n = weights[e][1]
+        pre = pre_s[e] + dot(hi, w_n) + dot(lo, w_n)
         gate = jax.nn.sigmoid(pre)
         value = (pre * gate).astype(BF)
         if e == 0:
-            out[own_rows, :] = value
+            o_own[...] = value
         else:
             o_mate[...] = value
         g = (cots[e].astype(F32) * gate * (1.0 + pre * (1.0 - gate))).astype(BF)
@@ -226,6 +264,7 @@
     u_m = send(u_all.at[0, 0], u_all.at[0, 1], mate)
     u_c = {k: send(u_all.at[0, 0], u_all.at[k, 0], (r, col_peer(k), d)) for k in peer_order(nc)}
     out_c = send(o_mate, out.at[own_rows], mate)
+    kept = bring(0, o_own, out.at[own_rows])
     for e in (1, 0):
         g = grads[e]
         w_part[e, 0:f, :] = dot(f_own, g, 0, 0)
@@ -241,8 +280,7 @@
         at = rows_at(owner, d if e == 0 else 1 - d)
         for q in range(nr):
             for h in range(2):
-                col = q * n + h * half
-                term = dot(u_all[k, e], dense[at, col : col + half])
+                term = dot(u_all[k, e], merged(at, (q * 2 + h) * hb, hb, hb))
                 g_acc[q, h] = term if first else g_acc[q, h] + term
 
     add_rows(0, 0, True)
@@ -271,10 +309,14 @@
         at = pl.ds(pl.multiple_of(col_peer(k) * wc, 8), wc)
         wc_c.append(send(w_2.at[at], w_cx.at[k], (r, col_peer(k), d)))
 
+    arrivals = list(reversed(peer_order(nc)))
     fwd_c = {}
-    for k in reversed(peer_order(nc)):
+    for i, k in enumerate(arrivals):
         u_c[k].wait_recv()
         fwd_c[k] = send(u_all.at[k, 0], u_all.at[k, 1], mate)
+        if i:
+            fwd_c[arrivals[i - 1]].wait_recv()
+            add_rows(arrivals[i - 1], 1, False)
         add_rows(k, 0, False)
 
     for copy in wc_c:
@@ -286,16 +328,13 @@
     wout[mine, :] = total * (1.0 / jnp.sqrt(jnp.full((1, 1), nr * nc * n, F32)))
     wg_c = [send(wout.at[mine], wout.at[mine], (r, col_peer(k), d)) for k in range(1, nc)]
 
-    for copy in fwd_c.values():
-        copy.wait_recv()
+    last = arrivals[-1]
+    fwd_c[last].wait_recv()
 
     def last_rows(owner, part):
-        col = pl.ds(pl.multiple_of(owner * n + part * half, half), half)
-        total = g_acc[owner, part]
-        for k in peer_order(nc):
-            at = rows_at(lax.rem(c - k + nc, nc), 1 - d)
-            total = total + dot(u_all[k, 1], dense[at, col])
-        return total
+        at = rows_at(lax.rem(c - last + nc, nc), 1 - d)
+        blocks = merged(at, (owner * 2 + part) * hb, hb, hb)
+        return g_acc[owner, part] + dot(u_all[last, 1], blocks)
 
     gx_c, gz_c = {}, {}
 
@@ -329,11 +368,28 @@
         total = total + gz_x[k].astype(F32)
     gfeat[...] = total.T.astype(BF)
 
+    kept.wait()
     out_c.wait_recv()
     for copy in ag_c:
         copy.wait_recv()
     for copy in made:
         copy.wait_send()
+
+
+def hand_out(out, gfeat, wout, out_o, gfeat_o, self_o, neigh_o, bias_o, sem):
+    f = self_o.shape[0]
+    pairs = [
+        (out, out_o),
+        (gfeat, gfeat_o),
+        (wout.at[pl.ds(0, f)], self_o),
+        (wout.at[pl.ds(f, f)], neigh_o),
+        (wout.at[pl.ds(2 * f, 1)], bias_o),
+    ]
+    copies = [pltpu.make_async_copy(a, b, sem.at[i]) for i, (a, b) in enumerate(pairs)]
+    for copy in copies:
+        copy.start()
+    for copy in copies:
+        copy.wait()
 
 
 def body(mesh, features, self_weight, neigh_weight, bias, cotangent, tile_values, tile_rows, tile_cols, tile_counts):
@@ -348,8 +404,10 @@
     w_rows = -(-(2 * f + 8) // unit) * unit
     chunks = 8
     width = max(slots, rb * cb)
-    copies = 12 + 5 * nr + 6 * nc
+    copies = 12 + 6 * nr + 6 * nc
     vmem = pl.BlockSpec(memory_space=pltpu.VMEM)
+    smem = pl.BlockSpec(memory_space=pltpu.SMEM)
+    hbm = pl.BlockSpec(memory_space=pl.ANY)
     dims = (nr, nc, n, block, slots, chunks)
     out, gfeat, wout = pl.pallas_call(
         functools.partial(kernel, dims),
@@ -358,14 +416,15 @@
             jax.ShapeDtypeStruct((half, f), BF),
             jax.ShapeDtypeStruct((w_rows, hh), F32),
         ),
-        in_specs=[vmem] * 7
-        + [pl.BlockSpec(memory_space=pltpu.SMEM), pl.BlockSpec(memory_space=pl.ANY)],
-        out_specs=(vmem, vmem, vmem),
+        in_specs=[hbm, hbm, hbm, vmem, hbm, vmem, vmem, smem, hbm],
+        out_specs=(hbm, vmem, vmem),
         scratch_shapes=[
             pltpu.VMEM((slots, block, block), BF),
             pltpu.VMEM((slots + 1, block, block), BF),
-            pltpu.VMEM((rb * block, cb * block), BF),
             pltpu.VMEM((nr * n, f), BF),
+            pltpu.VMEM((f, hh), BF),
+            pltpu.VMEM((f, hh), BF),
+            pltpu.VMEM((half, hh), BF),
             pltpu.VMEM((f, hh), BF),
             pltpu.VMEM((f, hh), BF),
             pltpu.VMEM((8, hh), F32),
@@ -378,6 +437,7 @@
             pltpu.VMEM((nc, half, f), F32),
             pltpu.VMEM((nc, half, f), BF),
             pltpu.VMEM((nc, half, f), BF),
+            pltpu.VMEM((half, hh), BF),
             pltpu.VMEM((half, hh), BF),
             pltpu.VMEM((nc, 2, f, half), BF),
             pltpu.VMEM((nr, 2, f, half), F32),
@@ -392,13 +452,14 @@
             pltpu.VMEM((w_rows // nr, hh), F32),
             pltpu.VMEM((nc, w_rows // nr // nc, hh), F32),
             pltpu.VMEM((f, half), F32),
+            pltpu.VMEM((2, half, hh), F32),
             pltpu.SemaphoreType.DMA((chunks,)),
-            pltpu.SemaphoreType.DMA((1,)),
+            pltpu.SemaphoreType.DMA((5,)),
             pltpu.SemaphoreType.DMA((copies,)),
             pltpu.SemaphoreType.DMA((copies,)),
         ],
         compiler_params=pltpu.CompilerParams(
-            collective_id=0, has_side_effects=True, vmem_limit_bytes=62 * 1024 * 1024
+            collective_id=0, has_side_effects=True, vmem_limit_bytes=60 * 1024 * 1024
         ),
         name="sage_layer",
     )(
@@ -412,7 +473,21 @@
         tile_counts,
         tile_values,
     )
-    return out, gfeat, wout[:f], wout[f : 2 * f], wout[2 * f]
+    out, gfeat, g_self, g_neigh, g_bias = pl.pallas_call(
+        hand_out,
+        out_shape=(
+            jax.ShapeDtypeStruct((n, hh), BF),
+            jax.ShapeDtypeStruct((half, f), BF),
+            jax.ShapeDtypeStruct((f, hh), F32),
+            jax.ShapeDtypeStruct((f, hh), F32),
+            jax.ShapeDtypeStruct((1, hh), F32),
+        ),
+        in_specs=[hbm] * 3,
+        out_specs=(hbm,) * 5,
+        scratch_shapes=[pltpu.SemaphoreType.DMA((5,))],
+        name="hand_out",
+    )(out, gfeat, wout)
+    return out, gfeat, g_self, g_neigh, g_bias.reshape(hh)
 
 
 def solution(mesh):

time: 51 us -> 54.1 us (1.061)
  Pallas kernels: 43.7 us -> 52.7 us
  local copies, waits for them, and re-layouts: 5.75 us -> 0 us
    pallas_call x0 -> x1, Pallas kernels: none -> 11.1 us  [body(): pl.pallas_call(hand_out, out_shape=(jax.ShapeDtypeStruct((n, hh), BF), ja...]
    unnamed x2 -> x0, local copies, waits for them, and re-layouts: 3.04 us -> none
    pallas_call x1, Pallas kernels: 43.7 us -> 41.6 us  [body(): pl.pallas_call(functools.partial(kernel, dims), out_shape=(jax.ShapeDtype...]
    slice x1 -> x0, local copies, waits for them, and re-layouts: 1.53 us -> none  [body(): return (out, gfeat, wout[:f], wout[f:2 * f], wout[2 * f])]
    squeeze x1 -> x0, local copies, waits for them, and re-layouts: 1.18 us -> none  [body(): return (out, gfeat, wout[:f], wout[f:2 * f], wout[2 * f])]
where the time goes in v2:
time: 54.1 us; the launch traced here: 54 us
  Pallas kernels  52.7 us (97%)
  between operations  1.29 us (2%)
    pallas_call x1, Pallas kernels, body(): pl.pallas_call(functools.partial(kernel, dims), out_shape=(jax.ShapeDtype...  41.6 us
    pallas_call x1, Pallas kernels, body(): pl.pallas_call(hand_out, out_shape=(jax.ShapeDtypeStruct((n, hh), BF), ja...  11.1 us

profile of v2, /device:TPU:0, one launch (start us, length us, event | category | flops | bytes accessed | tf_op | source)
XLA Modules:
  0.0 54.0 jit_solution(3346765769921708651)
XLA Ops:
  1.3 41.6 %sage_layer.1 = (bf16[512,128]{1,0:T(8,128)(2,1)}, bf16[256,128]{1,0:T(8,128)(2,1)}, f32[384,128]{1,0:T(8,128)}) custom-call(bf16[512,128]{1,0:T(8,128)(2,1)} %feat_hbm.1, bf16[128,128]{1,0:T(8,128)(2,1)} %ws_hbm.1, bf16[128,128]{1,0:T(8,128)(2,1)} %wn_hbm.1, f32[1,128]{1,0:T(1,128)} %bitcast.2, bf16[512,128]{1,0:T(8,128)(2,1)} %cot_hbm.1, ...), custom_call_target="tpu_custom_call" | custom-call | tf_op jit(solution)/shard_map/sage_layer/pallas_call | solution.py:412
  42.9 11.1 %hand_out.1 = (bf16[512,128]{1,0:T(8,128)(2,1)}, bf16[256,128]{1,0:T(8,128)(2,1)}, f32[128,128]{1,0:T(8,128)}, f32[128,128]{1,0:T(8,128)}, f32[1,128]{1,0:T(1,128)}) custom-call(bf16[512,128]{1,0:T(8,128)(2,1)} %get-tuple-element.13.out, bf16[256,128]{1,0:T(8,128)(2,1)} %get-tuple-element.14.gfeat, f32[384,128]{1,0:T(8,128)} %get-tuple-element.15.wout), custom_call_target="tpu_custom_call" | custom-call | tf_op jit(solution)/shard_map/hand_out/pallas_call | solution.py:476

commit v3 on v2

--- a/solution.py
+++ b/solution.py
@@ -67,6 +67,8 @@
     w_cx,
     v_t,
     pre_s,
+    hi_s,
+    g_s,
     tile_sem,
     loc_sem,
     send_sem,
@@ -128,7 +130,7 @@
         bring(0, feat_hbm, f_all.at[my_f]),
         bring(1, ws_hbm, ws),
         bring(2, wn_hbm, wn),
-        bring(3, cot_hbm.at[own_rows], cot),
+        bring(3, cot_hbm, cot),
     ]
 
     barrier = pltpu.get_barrier_semaphore()
@@ -157,16 +159,18 @@
     to_smem = pltpu.make_async_copy(idx_v, idx_s, loc_sem.at[4])
     to_smem.start()
 
+    for load in brought:
+        load.wait()
     pl.semaphore_wait(barrier, len(peers))
     biasb[...] = jnp.broadcast_to(bias[...], biasb.shape)
     feat_c = {
-        k: send(feat_hbm.at[own_rows], f_all.at[f_rows(0)], (row_peer(k), c, d))
+        k: send(f_all.at[f_rows(0)], f_all.at[f_rows(0)], (row_peer(k), c, d))
         for k in peer_order(nr)
     }
     early = [
-        send(ws_hbm, wsx, mate),
-        send(wn_hbm, wnx, mate),
-        send(cot_hbm.at[mate_rows], cotx, mate),
+        send(ws, wsx, mate),
+        send(wn, wnx, mate),
+        send(cot.at[mate_rows], cotx, mate),
         send(biasb, biasx, mate),
     ]
     run[slots] = jnp.zeros((block, block), BF)
@@ -189,47 +193,43 @@
         pair_c.append(send(f_all.at[f_rows(k)], f_all.at[f_rows(k)], mate))
     lax.fori_loop(slots // 2, slots, merge, acc, unroll=8)
 
-    def merged(first_row, first_col, height, width):
+    def merged(lines_at, first_col, width):
         lines = []
-        for i in range(height):
-            at = (first_row + i) * cb + first_col
-            line = [run[idx_s[2, at + j]] for j in range(width)]
+        for at in lines_at:
+            line = [run[idx_s[2, at * cb + first_col + j]] for j in range(width)]
             lines.append(jnp.concatenate(line, axis=1))
         return jnp.concatenate(lines, axis=0)
 
-    for load in brought:
-        load.wait()
     for copy in pair_c:
         copy.wait_recv()
 
-    hb = half // block
-
-    def rows_at(owner, part):
-        return (owner * 2 + part) * hb
-
-    def product(owner, part):
-        return dot(merged(rows_at(owner, part), 0, hb, cb), f_all[...])
+    part = half // 2
+    pb = part // block
+
+    def lines(owner, core, s):
+        return [((owner * 2 + core) * 2 + s) * pb + i for i in range(pb)]
 
     x_c, z_c = {}, {}
 
-    def finish(k):
-        x_c[k].wait_recv()
-        total = p_own[k] + p_x[k]
+    def finish(s, k):
+        x_c[s, k].wait_recv()
+        total = p_own[s, k] + p_x[s, k]
         if k == 0:
-            p_own[0] = total
+            p_own[s, 0] = total
         else:
-            s_b[k] = total.astype(BF)
-            z_c[k] = send(s_b.at[k], z_x.at[k], (r, col_peer(k), d))
-
-    order = peer_order(nc) + [0]
-    for i, k in enumerate(order):
+            s_b[s, k] = total.astype(BF)
+            z_c[s, k] = send(s_b.at[s, k], z_x.at[s, k], (r, col_peer(k), d))
+
+    steps = [(s, k) for s in range(2) for k in peer_order(nc) + [0]]
+    for i, (s, k) in enumerate(steps):
         owner = col_peer(k)
-        p_mate[k] = product(owner, 1 - d)
-        x_c[k] = send(p_mate.at[k], p_x.at[k], mate)
-        p_own[k] = product(owner, d)
+        both = dot(merged(lines(owner, 1 - d, s) + lines(owner, d, s), 0, cb), f_all[...])
+        p_mate[s, k] = both[:part]
+        x_c[s, k] = send(p_mate.at[s, k], p_x.at[s, k], mate)
+        p_own[s, k] = both[part:]
         if i:
-            finish(order[i - 1])
-    finish(order[-1])
+            finish(*steps[i - 1])
+    finish(*steps[-1])
     for copy in early:
         copy.wait_recv()
     f_own = f_all[f_rows(0), :]
@@ -237,34 +237,41 @@
     biases = [biasb[0:1, :], biasx[0:1, :]]
     for e in range(2):
         pre_s[e] = dot(f_own, weights[e][0]) + biases[e]
-    agg = p_own[0]
-    for k in peer_order(nc):
-        z_c[k].wait_recv()
-        agg = agg + z_x[k].astype(F32)
-
-    hi = agg.astype(BF)
-    lo = (agg - hi.astype(F32)).astype(BF)
-    cots = [cot[...], cotx[...]]
-    grads = []
-    u_t = v = None
-    for e in range(2):
-        w_n = weights[e][1]
-        pre = pre_s[e] + dot(hi, w_n) + dot(lo, w_n)
-        gate = jax.nn.sigmoid(pre)
-        value = (pre * gate).astype(BF)
-        if e == 0:
-            o_own[...] = value
-        else:
-            o_mate[...] = value
-        g = (cots[e].astype(F32) * gate * (1.0 + pre * (1.0 - gate))).astype(BF)
-        grads.append(g)
-        term = dot(w_n, g, 1, 1)
-        u_t = term if u_t is None else u_t + term
-    u_all[0, 0] = u_t.astype(BF)
-    u_m = send(u_all.at[0, 0], u_all.at[0, 1], mate)
-    u_c = {k: send(u_all.at[0, 0], u_all.at[k, 0], (r, col_peer(k), d)) for k in peer_order(nc)}
+
+    u_m, u_c = [], {}
+    for s in range(2):
+        at = slice(s * part, (s + 1) * part)
+        agg = p_own[s, 0]
+        for k in peer_order(nc):
+            z_c[s, k].wait_recv()
+            agg = agg + z_x[s, k].astype(F32)
+        hi = agg.astype(BF)
+        lo = (agg - hi.astype(F32)).astype(BF)
+        hi_s[at, :] = hi
+        u_t = None
+        for e in range(2):
+            w_n = weights[e][1]
+            pre = pre_s[e, at, :] + dot(hi, w_n) + dot(lo, w_n)
+            gate = jax.nn.sigmoid(pre)
+            value = (pre * gate).astype(BF)
+            if e == 0:
+                o_own[at, :] = value
+                ct = cot[pl.ds(pl.multiple_of(d * half + s * part, part), part), :]
+            else:
+                o_mate[at, :] = value
+                ct = cotx[at, :]
+            g = (ct.astype(F32) * gate * (1.0 + pre * (1.0 - gate))).astype(BF)
+            g_s[e, at, :] = g
+            term = dot(w_n, g, 1, 1)
+            u_t = term if u_t is None else u_t + term
+        u_all[s, 0, 0] = u_t.astype(BF)
+        for k in peer_order(nc):
+            u_c[s, k] = send(u_all.at[s, 0, 0], u_all.at[s, k, 0], (r, col_peer(k), d))
+        u_m.append(send(u_all.at[s, 0, 0], u_all.at[s, 0, 1], mate))
     out_c = send(o_mate, out.at[own_rows], mate)
     kept = bring(0, o_own, out.at[own_rows])
+    hi = hi_s[...]
+    grads = [g_s[0], g_s[1]]
     for e in (1, 0):
         g = grads[e]
         w_part[e, 0:f, :] = dot(f_own, g, 0, 0)
@@ -275,14 +282,18 @@
             w_c = send(w_part.at[1], w_x, mate)
     v_t[...] = dot(weights[0][0], grads[0], 1, 1) + dot(weights[1][0], grads[1], 1, 1)
 
-    def add_rows(k, e, first):
+    def rows_term(s, k, first_col):
         owner = lax.rem(c - k + nc, nc)
-        at = rows_at(owner, d if e == 0 else 1 - d)
+        left = jnp.concatenate([u_all[s, k, 0], u_all[s, k, 1]], axis=1)
+        return dot(left, merged(lines(owner, d, s) + lines(owner, 1 - d, s), first_col, 2 * pb))
+
+    def add_rows(s, k, first=False):
         for q in range(nr):
             for h in range(2):
-                term = dot(u_all[k, e], merged(at, (q * 2 + h) * hb, hb, hb))
+                term = rows_term(s, k, (q * 2 + h) * 2 * pb)
                 g_acc[q, h] = term if first else g_acc[q, h] + term
 
+    u_m[0].wait_recv()
     add_rows(0, 0, True)
 
     w_rows = w_x.shape[0]
@@ -295,8 +306,8 @@
         at = pl.ds(pl.multiple_of(row_peer(k) * wr, 8), wr)
         wr_c.append(send(w_part.at[0, at], w_rx.at[k], (row_peer(k), c, d)))
 
-    u_m.wait_recv()
-    add_rows(0, 1, False)
+    u_m[1].wait_recv()
+    add_rows(1, 0)
 
     for copy in wr_c:
         copy.wait_recv()
@@ -309,15 +320,14 @@
         at = pl.ds(pl.multiple_of(col_peer(k) * wc, 8), wc)
         wc_c.append(send(w_2.at[at], w_cx.at[k], (r, col_peer(k), d)))
 
-    arrivals = list(reversed(peer_order(nc)))
+    arrivals = [(s, k) for s in range(2) for k in peer_order(nc)]
     fwd_c = {}
-    for i, k in enumerate(arrivals):
-        u_c[k].wait_recv()
-        fwd_c[k] = send(u_all.at[k, 0], u_all.at[k, 1], mate)
+    for i, (s, k) in enumerate(arrivals):
+        u_c[s, k].wait_recv()
+        fwd_c[s, k] = send(u_all.at[s, k, 0], u_all.at[s, k, 1], mate)
         if i:
             fwd_c[arrivals[i - 1]].wait_recv()
-            add_rows(arrivals[i - 1], 1, False)
-        add_rows(k, 0, False)
+            add_rows(*arrivals[i - 1])
 
     for copy in wc_c:
         copy.wait_recv()
@@ -331,10 +341,8 @@
     last = arrivals[-1]
     fwd_c[last].wait_recv()
 
-    def last_rows(owner, part):
-        at = rows_at(lax.rem(c - last + nc, nc), 1 - d)
-        blocks = merged(at, (owner * 2 + part) * hb, hb, hb)
-        return g_acc[owner, part] + dot(u_all[last, 1], blocks)
+    def last_rows(owner, core):
+        return g_acc[owner, core] + rows_term(*last, (owner * 2 + core) * 2 * pb)
 
     gx_c, gz_c = {}, {}
 
@@ -376,20 +384,13 @@
         copy.wait_send()
 
 
-def hand_out(out, gfeat, wout, out_o, gfeat_o, self_o, neigh_o, bias_o, sem):
+def hand_out(out, gfeat, wout, out_o, gfeat_o, self_o, neigh_o, bias_o):
     f = self_o.shape[0]
-    pairs = [
-        (out, out_o),
-        (gfeat, gfeat_o),
-        (wout.at[pl.ds(0, f)], self_o),
-        (wout.at[pl.ds(f, f)], neigh_o),
-        (wout.at[pl.ds(2 * f, 1)], bias_o),
-    ]
-    copies = [pltpu.make_async_copy(a, b, sem.at[i]) for i, (a, b) in enumerate(pairs)]
-    for copy in copies:
-        copy.start()
-    for copy in copies:
-        copy.wait()
+    out_o[...] = out[...]
+    gfeat_o[...] = gfeat[...]
+    self_o[...] = wout[0:f, :]
+    neigh_o[...] = wout[f : 2 * f, :]
+    bias_o[...] = wout[2 * f : 2 * f + 1, :]
 
 
 def body(mesh, features, self_weight, neigh_weight, bias, cotangent, tile_values, tile_rows, tile_cols, tile_counts):
@@ -404,7 +405,7 @@
     w_rows = -(-(2 * f + 8) // unit) * unit
     chunks = 8
     width = max(slots, rb * cb)
-    copies = 12 + 6 * nr + 6 * nc
+    copies = 12 + 6 * nr + 9 * nc
     vmem = pl.BlockSpec(memory_space=pltpu.VMEM)
     smem = pl.BlockSpec(memory_space=pltpu.SMEM)
     hbm = pl.BlockSpec(memory_space=pl.ANY)
@@ -424,7 +425,7 @@
             pltpu.VMEM((nr * n, f), BF),
             pltpu.VMEM((f, hh), BF),
             pltpu.VMEM((f, hh), BF),
-            pltpu.VMEM((half, hh), BF),
+            pltpu.VMEM((n, hh), BF),
             pltpu.VMEM((f, hh), BF),
             pltpu.VMEM((f, hh), BF),
             pltpu.VMEM((8, hh), F32),
@@ -432,14 +433,14 @@
             pltpu.VMEM((half, hh), BF),
             pltpu.VMEM((8, width), jnp.int32),
             pltpu.SMEM((8, width), jnp.int32),
-            pltpu.VMEM((nc, half, f), F32),
-            pltpu.VMEM((nc, half, f), F32),
-            pltpu.VMEM((nc, half, f), F32),
-            pltpu.VMEM((nc, half, f), BF),
-            pltpu.VMEM((nc, half, f), BF),
+            pltpu.VMEM((2, nc, half // 2, f), F32),
+            pltpu.VMEM((2, nc, half // 2, f), F32),
+            pltpu.VMEM((2, nc, half // 2, f), F32),
+            pltpu.VMEM((2, nc, half // 2, f), BF),
+            pltpu.VMEM((2, nc, half // 2, f), BF),
             pltpu.VMEM((half, hh), BF),
             pltpu.VMEM((half, hh), BF),
-            pltpu.VMEM((nc, 2, f, half), BF),
+            pltpu.VMEM((2, nc, 2, f, half // 2), BF),
             pltpu.VMEM((nr, 2, f, half), F32),
             pltpu.VMEM((nr, f, half), F32),
             pltpu.VMEM((nr, f, half), F32),
@@ -453,6 +454,8 @@
             pltpu.VMEM((nc, w_rows // nr // nc, hh), F32),
             pltpu.VMEM((f, half), F32),
             pltpu.VMEM((2, half, hh), F32),
+            pltpu.VMEM((half, f), BF),
+            pltpu.VMEM((2, half, hh), BF),
             pltpu.SemaphoreType.DMA((chunks,)),
             pltpu.SemaphoreType.DMA((5,)),
             pltpu.SemaphoreType.DMA((copies,)),
@@ -482,9 +485,8 @@
             jax.ShapeDtypeStruct((f, hh), F32),
             jax.ShapeDtypeStruct((1, hh), F32),
         ),
-        in_specs=[hbm] * 3,
-        out_specs=(hbm,) * 5,
-        scratch_shapes=[pltpu.SemaphoreType.DMA((5,))],
+        in_specs=[vmem] * 3,
+        out_specs=(vmem,) * 5,
         name="hand_out",
     )(out, gfeat, wout)
     return out, gfeat, g_self, g_neigh, g_bias.reshape(hh)

time: 54.1 us -> 46.6 us (0.86)
  Pallas kernels: 52.7 us -> 45.2 us
    pallas_call x1, Pallas kernels: 11.1 us -> 1.75 us  [body(): pl.pallas_call(hand_out, out_shape=(jax.ShapeDtypeStruct((n, hh), BF), ja...]
    pallas_call x1, Pallas kernels: 41.6 us -> 43.4 us  [body(): pl.pallas_call(functools.partial(kernel, dims), out_shape=(jax.ShapeDtype...]
where the time goes in v3:
time: 46.6 us; the launch traced here: 46.5 us
  Pallas kernels  45.2 us (97%)
  between operations  1.29 us (3%)
    pallas_call x1, Pallas kernels, body(): pl.pallas_call(functools.partial(kernel, dims), out_shape=(jax.ShapeDtype...  43.4 us
    pallas_call x1, Pallas kernels, body(): pl.pallas_call(hand_out, out_shape=(jax.ShapeDtypeStruct((n, hh), BF), ja...  1.75 us

profile of v3, /device:TPU:0, one launch (start us, length us, event | category | flops | bytes accessed | tf_op | source)
XLA Modules:
  0.0 46.5 jit_solution(5535051302419122373)
XLA Ops:
  1.3 43.4 %sage_layer.1 = (bf16[512,128]{1,0:T(8,128)(2,1)}, bf16[256,128]{1,0:T(8,128)(2,1)}, f32[384,128]{1,0:T(8,128)}) custom-call(bf16[512,128]{1,0:T(8,128)(2,1)} %feat_hbm.1, bf16[128,128]{1,0:T(8,128)(2,1)} %ws_hbm.1, bf16[128,128]{1,0:T(8,128)(2,1)} %wn_hbm.1, f32[1,128]{1,0:T(1,128)} %bitcast.2, bf16[512,128]{1,0:T(8,128)(2,1)} %cot_hbm.1, ...), custom_call_target="tpu_custom_call" | custom-call | tf_op jit(solution)/shard_map/sage_layer/pallas_call | solution.py:413
  44.7 1.8 %hand_out.1 = (bf16[512,128]{1,0:T(8,128)(2,1)}, bf16[256,128]{1,0:T(8,128)(2,1)}, f32[128,128]{1,0:T(8,128)}, f32[128,128]{1,0:T(8,128)}, f32[1,128]{1,0:T(1,128)}) custom-call(bf16[512,128]{1,0:T(8,128)(2,1)} %get-tuple-element.13.out, bf16[256,128]{1,0:T(8,128)(2,1)} %get-tuple-element.14.gfeat, f32[384,128]{1,0:T(8,128)} %get-tuple-element.15.wout), custom_call_target="tpu_custom_call" | custom-call | tf_op jit(solution)/shard_map/hand_out/pallas_call | solution.py:479

commit v4 on v3

--- a/solution.py
+++ b/solution.py
@@ -105,6 +105,26 @@
         made.append(copy)
         return copy
 
+    my_f = pl.ds(pl.multiple_of(r * n, n), n)
+    own_rows = pl.ds(pl.multiple_of(d * half, half), half)
+    mate_rows = pl.ds(pl.multiple_of((1 - d) * half, half), half)
+
+    def f_rows(k):
+        at = lax.rem(r - k + nr, nr) * n + d * half
+        return pl.ds(pl.multiple_of(at, half), half)
+
+    def bring(i, src, dst):
+        load = pltpu.make_async_copy(src, dst, loc_sem.at[i])
+        load.start()
+        return load
+
+    brought = [
+        bring(0, feat_hbm, f_all.at[my_f]),
+        bring(1, ws_hbm, ws),
+        bring(2, wn_hbm, wn),
+        bring(3, cot_hbm, cot),
+    ]
+
     per = slots // chunks
     loads = []
     for i in range(chunks):
@@ -112,26 +132,6 @@
         load = pltpu.make_async_copy(tiles_hbm.at[part], tiles.at[part], tile_sem.at[i])
         load.start()
         loads.append(load)
-
-    my_f = pl.ds(pl.multiple_of(r * n, n), n)
-    own_rows = pl.ds(pl.multiple_of(d * half, half), half)
-    mate_rows = pl.ds(pl.multiple_of((1 - d) * half, half), half)
-
-    def f_rows(k):
-        at = lax.rem(r - k + nr, nr) * n + d * half
-        return pl.ds(pl.multiple_of(at, half), half)
-
-    def bring(i, src, dst):
-        load = pltpu.make_async_copy(src, dst, loc_sem.at[i])
-        load.start()
-        return load
-
-    brought = [
-        bring(0, feat_hbm, f_all.at[my_f]),
-        bring(1, ws_hbm, ws),
-        bring(2, wn_hbm, wn),
-        bring(3, cot_hbm, cot),
-    ]
 
     barrier = pltpu.get_barrier_semaphore()
     peers = [mate]
@@ -328,15 +328,20 @@
         if i:
             fwd_c[arrivals[i - 1]].wait_recv()
             add_rows(*arrivals[i - 1])
-
-    for copy in wc_c:
-        copy.wait_recv()
-    total = w_2[pl.ds(pl.multiple_of(c * wc, 8), wc), :]
-    for k in range(1, nc):
-        total = total + w_cx[k]
-    mine = pl.ds(pl.multiple_of(r * wr + c * wc, 8), wc)
-    wout[mine, :] = total * (1.0 / jnp.sqrt(jnp.full((1, 1), nr * nc * n, F32)))
-    wg_c = [send(wout.at[mine], wout.at[mine], (r, col_peer(k), d)) for k in range(1, nc)]
+        if i == 1:
+            for copy in wc_c:
+                copy.wait_recv()
+            total = w_2[pl.ds(pl.multiple_of(c * wc, 8), wc), :]
+            for k in range(1, nc):
+                total = total + w_cx[k]
+            mine = pl.ds(pl.multiple_of(r * wr + c * wc, 8), wc)
+            wout[mine, :] = total * (1.0 / jnp.sqrt(jnp.full((1, 1), nr * nc * n, F32)))
+            wg_c = [send(wout.at[mine], wout.at[mine], (r, col_peer(k), d)) for k in range(1, nc)]
+        if i == len(arrivals) - 2:
+            for copy in wg_c:
+                copy.wait_recv()
+            whole = pl.ds(pl.multiple_of(r * wr, 8), wr)
+            ag_c = [send(wout.at[whole], wout.at[whole], (row_peer(k), c, d)) for k in range(1, nr)]
 
     last = arrivals[-1]
     fwd_c[last].wait_recv()
@@ -364,11 +369,6 @@
         if i:
             finish_back(order[i - 1])
     finish_back(order[-1])
-
-    for copy in wg_c:
-        copy.wait_recv()
-    whole = pl.ds(pl.multiple_of(r * wr, 8), wr)
-    ag_c = [send(wout.at[whole], wout.at[whole], (row_peer(k), c, d)) for k in range(1, nr)]
 
     total = v_t[...] + g_own[0]
     for k in peer_order(nr):

time: 46.6 us -> 49.1 us (1.054)
  Pallas kernels: 45.2 us -> 47.6 us
    pallas_call x1, Pallas kernels: 43.4 us -> 45.9 us  [body(): pl.pallas_call(functools.partial(kernel, dims), out_shape=(jax.ShapeDtype...]
where the time goes in v4:
time: 49.1 us; the launch traced here: 48.9 us
  Pallas kernels  47.6 us (97%)
  between operations  1.29 us (3%)
    pallas_call x1, Pallas kernels, body(): pl.pallas_call(functools.partial(kernel, dims), out_shape=(jax.ShapeDtype...  45.9 us
    pallas_call x1, Pallas kernels, body(): pl.pallas_call(hand_out, out_shape=(jax.ShapeDtypeStruct((n, hh), BF), ja...  1.75 us

profile of v4, /device:TPU:0, one launch (start us, length us, event | category | flops | bytes accessed | tf_op | source)
XLA Modules:
  0.0 48.9 jit_solution(14732010344143096205)
XLA Ops:
  1.3 45.9 %sage_layer.1 = (bf16[512,128]{1,0:T(8,128)(2,1)}, bf16[256,128]{1,0:T(8,128)(2,1)}, f32[384,128]{1,0:T(8,128)}) custom-call(bf16[512,128]{1,0:T(8,128)(2,1)} %feat_hbm.1, bf16[128,128]{1,0:T(8,128)(2,1)} %ws_hbm.1, bf16[128,128]{1,0:T(8,128)(2,1)} %wn_hbm.1, f32[1,128]{1,0:T(1,128)} %bitcast.2, bf16[512,128]{1,0:T(8,128)(2,1)} %cot_hbm.1, ...), custom_call_target="tpu_custom_call" | custom-call | tf_op jit(solution)/shard_map/sage_layer/pallas_call | solution.py:413
  47.1 1.8 %hand_out.1 = (bf16[512,128]{1,0:T(8,128)(2,1)}, bf16[256,128]{1,0:T(8,128)(2,1)}, f32[128,128]{1,0:T(8,128)}, f32[128,128]{1,0:T(8,128)}, f32[1,128]{1,0:T(1,128)}) custom-call(bf16[512,128]{1,0:T(8,128)(2,1)} %get-tuple-element.13.out, bf16[256,128]{1,0:T(8,128)(2,1)} %get-tuple-element.14.gfeat, f32[384,128]{1,0:T(8,128)} %get-tuple-element.15.wout), custom_call_target="tpu_custom_call" | custom-call | tf_op jit(solution)/shard_map/hand_out/pallas_call | solution.py:479

commit v5 on v2

--- a/solution.py
+++ b/solution.py
@@ -138,6 +138,19 @@
     for p in peers:
         pl.semaphore_signal(barrier, inc=1, device_id=p, device_id_type=pl.DeviceIdType.MESH)
 
+    pl.semaphore_wait(barrier, len(peers))
+    biasb[...] = jnp.broadcast_to(bias[...], biasb.shape)
+    feat_c = {
+        k: send(feat_hbm.at[own_rows], f_all.at[f_rows(0)], (row_peer(k), c, d))
+        for k in peer_order(nr)
+    }
+    early = [
+        send(ws_hbm, wsx, mate),
+        send(wn_hbm, wnx, mate),
+        send(cot_hbm.at[mate_rows], cotx, mate),
+        send(biasb, biasx, mate),
+    ]
+
     live = counts[0]
     lane = lax.broadcasted_iota(jnp.int32, (slots, slots), 1)
     sub = lax.broadcasted_iota(jnp.int32, (slots, slots), 0)
@@ -157,18 +170,6 @@
     to_smem = pltpu.make_async_copy(idx_v, idx_s, loc_sem.at[4])
     to_smem.start()
 
-    pl.semaphore_wait(barrier, len(peers))
-    biasb[...] = jnp.broadcast_to(bias[...], biasb.shape)
-    feat_c = {
-        k: send(feat_hbm.at[own_rows], f_all.at[f_rows(0)], (row_peer(k), c, d))
-        for k in peer_order(nr)
-    }
-    early = [
-        send(ws_hbm, wsx, mate),
-        send(wn_hbm, wnx, mate),
-        send(cot_hbm.at[mate_rows], cotx, mate),
-        send(biasb, biasx, mate),
-    ]
     run[slots] = jnp.zeros((block, block), BF)
     w_part[...] = jnp.zeros_like(w_part)
     to_smem.wait()
@@ -182,12 +183,12 @@
         return acc
 
     acc = jnp.zeros((block, block), F32)
-    acc = lax.fori_loop(0, slots // 2, merge, acc, unroll=8)
+    acc = lax.fori_loop(0, slots // 2, merge, acc, unroll=16)
     pair_c = []
     for k in peer_order(nr):
         feat_c[k].wait_recv()
         pair_c.append(send(f_all.at[f_rows(k)], f_all.at[f_rows(k)], mate))
-    lax.fori_loop(slots // 2, slots, merge, acc, unroll=8)
+    lax.fori_loop(slots // 2, slots, merge, acc, unroll=16)
 
     def merged(first_row, first_col, height, width):
         lines = []
@@ -298,17 +299,6 @@
     u_m.wait_recv()
     add_rows(0, 1, False)
 
-    for copy in wr_c:
-        copy.wait_recv()
-    total = w_part[0, pl.ds(pl.multiple_of(r * wr, 8), wr), :]
-    for k in range(1, nr):
-        total = total + w_rx[k]
-    w_2[...] = total
-    wc_c = []
-    for k in range(1, nc):
-        at = pl.ds(pl.multiple_of(col_peer(k) * wc, 8), wc)
-        wc_c.append(send(w_2.at[at], w_cx.at[k], (r, col_peer(k), d)))
-
     arrivals = list(reversed(peer_order(nc)))
     fwd_c = {}
     for i, k in enumerate(arrivals):
@@ -318,6 +308,17 @@
             fwd_c[arrivals[i - 1]].wait_recv()
             add_rows(arrivals[i - 1], 1, False)
         add_rows(k, 0, False)
+        if i == 0:
+            for copy in wr_c:
+                copy.wait_recv()
+            total = w_part[0, pl.ds(pl.multiple_of(r * wr, 8), wr), :]
+            for k in range(1, nr):
+                total = total + w_rx[k]
+            w_2[...] = total
+            wc_c = []
+            for k in range(1, nc):
+                at = pl.ds(pl.multiple_of(col_peer(k) * wc, 8), wc)
+                wc_c.append(send(w_2.at[at], w_cx.at[k], (r, col_peer(k), d)))
 
     for copy in wc_c:
         copy.wait_recv()
@@ -376,20 +377,13 @@
         copy.wait_send()
 
 
-def hand_out(out, gfeat, wout, out_o, gfeat_o, self_o, neigh_o, bias_o, sem):
+def hand_out(out, gfeat, wout, out_o, gfeat_o, self_o, neigh_o, bias_o):
     f = self_o.shape[0]
-    pairs = [
-        (out, out_o),
-        (gfeat, gfeat_o),
-        (wout.at[pl.ds(0, f)], self_o),
-        (wout.at[pl.ds(f, f)], neigh_o),
-        (wout.at[pl.ds(2 * f, 1)], bias_o),
-    ]
-    copies = [pltpu.make_async_copy(a, b, sem.at[i]) for i, (a, b) in enumerate(pairs)]
-    for copy in copies:
-        copy.start()
-    for copy in copies:
-        copy.wait()
+    out_o[...] = out[...]
+    gfeat_o[...] = gfeat[...]
+    self_o[...] = wout[0:f, :]
+    neigh_o[...] = wout[f : 2 * f, :]
+    bias_o[...] = wout[2 * f : 2 * f + 1, :]
 
 
 def body(mesh, features, self_weight, neigh_weight, bias, cotangent, tile_values, tile_rows, tile_cols, tile_counts):
@@ -482,9 +476,8 @@
             jax.ShapeDtypeStruct((f, hh), F32),
             jax.ShapeDtypeStruct((1, hh), F32),
         ),
-        in_specs=[hbm] * 3,
-        out_specs=(hbm,) * 5,
-        scratch_shapes=[pltpu.SemaphoreType.DMA((5,))],
+        in_specs=[vmem] * 3,
+        out_specs=(vmem,) * 5,
         name="hand_out",
     )(out, gfeat, wout)
     return out, gfeat, g_self, g_neigh, g_bias.reshape(hh)

time: 54.1 us -> 45.2 us (0.84)
  Pallas kernels: 52.7 us -> 43.7 us
    pallas_call x1, Pallas kernels: 11.1 us -> 1.75 us  [body(): pl.pallas_call(hand_out, out_shape=(jax.ShapeDtypeStruct((n, hh), BF), ja...]
where the time goes in v5:
time: 45.2 us; the launch traced here: 45 us
  Pallas kernels  43.7 us (97%)
  between operations  1.29 us (3%)
    pallas_call x1, Pallas kernels, body(): pl.pallas_call(functools.partial(kernel, dims), out_shape=(jax.ShapeDtype...  42 us
    pallas_call x1, Pallas kernels, body(): pl.pallas_call(hand_out, out_shape=(jax.ShapeDtypeStruct((n, hh), BF), ja...  1.75 us

profile of v5, /device:TPU:0, one launch (start us, length us, event | category | flops | bytes accessed | tf_op | source)
XLA Modules:
  0.0 45.0 jit_solution(11080155454143038331)
XLA Ops:
  1.3 42.0 %sage_layer.1 = (bf16[512,128]{1,0:T(8,128)(2,1)}, bf16[256,128]{1,0:T(8,128)(2,1)}, f32[384,128]{1,0:T(8,128)}) custom-call(bf16[512,128]{1,0:T(8,128)(2,1)} %feat_hbm.1, bf16[128,128]{1,0:T(8,128)(2,1)} %ws_hbm.1, bf16[128,128]{1,0:T(8,128)(2,1)} %wn_hbm.1, f32[1,128]{1,0:T(1,128)} %bitcast.2, bf16[512,128]{1,0:T(8,128)(2,1)} %cot_hbm.1, ...), custom_call_target="tpu_custom_call" | custom-call | tf_op jit(solution)/shard_map/sage_layer/pallas_call | solution.py:406
  43.3 1.8 %hand_out.1 = (bf16[512,128]{1,0:T(8,128)(2,1)}, bf16[256,128]{1,0:T(8,128)(2,1)}, f32[128,128]{1,0:T(8,128)}, f32[128,128]{1,0:T(8,128)}, f32[1,128]{1,0:T(1,128)}) custom-call(bf16[512,128]{1,0:T(8,128)(2,1)} %get-tuple-element.13.out, bf16[256,128]{1,0:T(8,128)(2,1)} %get-tuple-element.14.gfeat, f32[384,128]{1,0:T(8,128)} %get-tuple-element.15.wout), custom_call_target="tpu_custom_call" | custom-call | tf_op jit(solution)/shard_map/hand_out/pallas_call | solution.py:470

commit v6 on v2

--- a/solution.py
+++ b/solution.py
@@ -376,20 +376,13 @@
         copy.wait_send()
 
 
-def hand_out(out, gfeat, wout, out_o, gfeat_o, self_o, neigh_o, bias_o, sem):
+def hand_out(out, gfeat, wout, out_o, gfeat_o, self_o, neigh_o, bias_o):
     f = self_o.shape[0]
-    pairs = [
-        (out, out_o),
-        (gfeat, gfeat_o),
-        (wout.at[pl.ds(0, f)], self_o),
-        (wout.at[pl.ds(f, f)], neigh_o),
-        (wout.at[pl.ds(2 * f, 1)], bias_o),
-    ]
-    copies = [pltpu.make_async_copy(a, b, sem.at[i]) for i, (a, b) in enumerate(pairs)]
-    for copy in copies:
-        copy.start()
-    for copy in copies:
-        copy.wait()
+    out_o[...] = out[...]
+    gfeat_o[...] = gfeat[...]
+    self_o[...] = wout[0:f, :]
+    neigh_o[...] = wout[f : 2 * f, :]
+    bias_o[...] = wout[2 * f : 2 * f + 1, :]
 
 
 def body(mesh, features, self_weight, neigh_weight, bias, cotangent, tile_values, tile_rows, tile_cols, tile_counts):
@@ -482,9 +475,8 @@
             jax.ShapeDtypeStruct((f, hh), F32),
             jax.ShapeDtypeStruct((1, hh), F32),
         ),
-        in_specs=[hbm] * 3,
-        out_specs=(hbm,) * 5,
-        scratch_shapes=[pltpu.SemaphoreType.DMA((5,))],
+        in_specs=[vmem] * 3,
+        out_specs=(vmem,) * 5,
         name="hand_out",
     )(out, gfeat, wout)
     return out, gfeat, g_self, g_neigh, g_bias.reshape(hh)

time: 54.1 us -> 44.8 us (0.83)
  Pallas kernels: 52.7 us -> 43.3 us
    pallas_call x1, Pallas kernels: 11.1 us -> 1.75 us  [body(): pl.pallas_call(hand_out, out_shape=(jax.ShapeDtypeStruct((n, hh), BF), ja...]
where the time goes in v6:
time: 44.8 us; the launch traced here: 44.6 us
  Pallas kernels  43.3 us (97%)
  between operations  1.29 us (3%)
    pallas_call x1, Pallas kernels, body(): pl.pallas_call(functools.partial(kernel, dims), out_shape=(jax.ShapeDtype...  41.6 us
    pallas_call x1, Pallas kernels, body(): pl.pallas_call(hand_out, out_shape=(jax.ShapeDtypeStruct((n, hh), BF), ja...  1.75 us

profile of v6, /device:TPU:0, one launch (start us, length us, event | category | flops | bytes accessed | tf_op | source)
XLA Modules:
  0.0 44.6 jit_solution(13116409826213847686)
XLA Ops:
  1.3 41.6 %sage_layer.1 = (bf16[512,128]{1,0:T(8,128)(2,1)}, bf16[256,128]{1,0:T(8,128)(2,1)}, f32[384,128]{1,0:T(8,128)}) custom-call(bf16[512,128]{1,0:T(8,128)(2,1)} %feat_hbm.1, bf16[128,128]{1,0:T(8,128)(2,1)} %ws_hbm.1, bf16[128,128]{1,0:T(8,128)(2,1)} %wn_hbm.1, f32[1,128]{1,0:T(1,128)} %bitcast.2, bf16[512,128]{1,0:T(8,128)(2,1)} %cot_hbm.1, ...), custom_call_target="tpu_custom_call" | custom-call | tf_op jit(solution)/shard_map/sage_layer/pallas_call | solution.py:405
  42.9 1.8 %hand_out.1 = (bf16[512,128]{1,0:T(8,128)(2,1)}, bf16[256,128]{1,0:T(8,128)(2,1)}, f32[128,128]{1,0:T(8,128)}, f32[128,128]{1,0:T(8,128)}, f32[1,128]{1,0:T(1,128)}) custom-call(bf16[512,128]{1,0:T(8,128)(2,1)} %get-tuple-element.13.out, bf16[256,128]{1,0:T(8,128)(2,1)} %get-tuple-element.14.gfeat, f32[384,128]{1,0:T(8,128)} %get-tuple-element.15.wout), custom_call_target="tpu_custom_call" | custom-call | tf_op jit(solution)/shard_map/hand_out/pallas_call | solution.py:469
